TPU v7x, 256 devices: a whole 4x4x8 slice. The times are simulated.
256 devices in a mesh: member: 8 (over x, core), band: 32 (over z, y).
Axes of the slice: x: 4, y: 4, z: 8, core: 2. Of those that a mesh axis runs over, the one named last changes fastest.
Arguments:
- grid: float32 [384, 640, 1280], P('member', 'band'), parts along dimension 0, may hold values from -6 to 6
- row_points: int32 [640], replicated, may hold values from 20 to 1280, as said below
- row_latitude: int32 [640], replicated, may hold values from 0 to 639, as said below
- order_owner: int32 [320], replicated, may hold values from 0 to 31, as said below
- legendre: bfloat16 [640, 320, 320], P('band'), may hold values from -6 to 6
Outputs:
- spectral: float32 [640, 2, 384, 320], P('band', None, 'member'), parts along dimension 2
- energy: float32 [384, 320], P('member'), parts along dimension 0
There are 8 independent parts, one for each index of `member`. A program takes and returns all parts, laid end to end along the dimension named above; an argument that names none is the same for every part. Nothing has to cross between parts.
Inputs may be any that keep to these rules, and one draw needn't show every extreme that they name: row_points is the same for a row and its mirror row 639-l, never falls from a pole towards the equator, is a multiple of 4, is 20 at the pole rows and equals 1280 at the equator rows. row_latitude is a permutation; the first 320 stored rows hold northern latitudes, and stored row 639-r holds the mirror 640 - 1-l of the latitude l of stored row r. order_owner never falls with the order; each device owns at most 20 orders, and one device owns exactly 20 in every draw.
All inputs are finite; a program needn't handle non-finite values.
Results may differ from a plain program's by a relative error of at most 0.0029.
Values may be sent and summed in bfloat16 or wider, within the bound.
A program may use at most 256 MiB of HBM per device.

v0:
```python
import math

import jax
import jax.numpy as jnp
from jax import lax
from jax.sharding import PartitionSpec as P

NN = 320
NLONMAX = 1280


def fourier_row(row_values, length):
    columns = jnp.arange(NLONMAX, dtype=jnp.int32)
    orders = jnp.arange(NN, dtype=jnp.int32)
    phase = orders[:, None] * columns[None, :] % length
    length_real = length.astype(jnp.float32)
    angle = phase.astype(jnp.float32) * (2.0 * math.pi / length_real)
    keep = (columns[None, :] < length) & (orders[:, None] <= (length - 1) // 2)
    weight = jnp.where(keep, 1.0 / length_real, jnp.zeros((), jnp.float32))
    table = jnp.concatenate([jnp.cos(angle) * weight, -jnp.sin(angle) * weight], axis=0)
    result = lax.dot_general(
        table,
        row_values,
        (((1,), (1,)), ((), ())),
        precision=lax.Precision.HIGHEST,
        preferred_element_type=jnp.float32,
    )
    field_count = row_values.shape[0]
    return result.reshape(2, NN, field_count).transpose(1, 0, 2).reshape(NN, 2 * field_count)


def owned_orders(order_owner, owners, ranks):
    orders = jnp.arange(NN, dtype=jnp.int32)
    local = order_owner[None, :] == owners[:, None]
    position = jnp.cumsum(local.astype(jnp.int32), axis=1) - 1
    match = local & (position == ranks[:, None])
    slot_order = jnp.sum(jnp.where(match, orders[None, :], 0), axis=1)
    valid = jnp.any(match, axis=1)
    return (slot_order, valid)


def on_device(grid, row_points, row_latitude, order_owner, legendre):
    field_count = grid.shape[0]
    row_count = grid.shape[1]
    capacity = legendre.shape[0]
    total_rows = row_latitude.shape[0]
    half_rows = total_rows // 2
    band_count = lax.axis_size("band")
    device = lax.axis_index("band")
    local_latitude = lax.dynamic_slice_in_dim(row_latitude, device * row_count, row_count)
    local_length = jnp.take(row_points, local_latitude)

    def transform_row(row_index):
        row_values = lax.dynamic_index_in_dim(grid, row_index, 1, keepdims=False)
        return fourier_row(row_values, local_length[row_index])

    fourier = lax.map(transform_row, jnp.arange(row_count, dtype=jnp.int32)).astype(jnp.bfloat16)
    slot_ranks = jnp.arange(capacity, dtype=jnp.int32)
    slot_order, valid = owned_orders(
        order_owner, jnp.zeros((capacity,), jnp.int32) + device, slot_ranks
    )
    degrees = jnp.arange(NN, dtype=jnp.int32)
    parity = jnp.where((degrees[None, :] + slot_order[:, None]) % 2 == 0, 1.0, -1.0).astype(
        jnp.bfloat16
    )
    slot_ids = jnp.arange(band_count * capacity, dtype=jnp.int32)
    send_order, send_valid = owned_orders(order_owner, slot_ids // capacity, slot_ids % capacity)
    by_order = jnp.transpose(fourier, (1, 0, 2)).reshape(NN, row_count * 2 * field_count)
    packed = jnp.where(
        send_valid[:, None], jnp.take(by_order, send_order, axis=0), jnp.zeros((), jnp.bfloat16)
    )
    received = lax.all_to_all(packed, "band", split_axis=0, concat_axis=1, tiled=True)
    selected = received.reshape(capacity, total_rows, 2 * field_count)
    column = jnp.where(row_latitude < half_rows, row_latitude, total_rows - 1 - row_latitude)
    southern = row_latitude >= half_rows
    gathered = jnp.take(legendre, column, axis=2)
    signed = jnp.where(southern[None, None, :], gathered * parity[:, :, None], gathered)
    summed = jnp.einsum("srk,snr->skn", selected, signed, preferred_element_type=jnp.float32)
    keep = (degrees[None, :] >= slot_order[:, None]) & valid[:, None]
    summed = jnp.where(keep[:, None, :], summed, jnp.zeros((), jnp.float32))
    spectral = summed.reshape(capacity, 2, field_count, NN)
    weight = jnp.where(valid, jnp.where(slot_order == 0, 1.0, 2.0), 0.0).astype(jnp.float32)
    local_power = jnp.einsum(
        "scfn,s->fn", spectral * spectral, weight, precision=lax.Precision.HIGHEST
    )
    power = lax.psum(local_power, "band")
    energy = power / (2 * degrees + 1).astype(jnp.float32)
    return (spectral, energy)


def solution(mesh):
    in_specs = (P("member", "band", None), P(), P(), P(), P("band", None, None))
    out_specs = (P("band", None, "member", None), P("member", None))
    return jax.shard_map(
        on_device, mesh=mesh, in_specs=in_specs, out_specs=out_specs, check_vma=False
    )
```

profile of v0, /device:TPU:2, one launch (start us, length us, event | category | flops | bytes accessed | tf_op | source)
XLA Modules:
  0.0 919.2 jit_solution(8152856281914859953)
XLA Ops:
  4.4 667.7 %while.13 = (s32[]{:T(128)}, bf16[20,320,96]{1,2,0:T(8,128)(2,1)S(1)}, s32[20]{0:T(128)S(1)}, s32[20]{0:T(128)S(1)}, f32[48,20,1280]{2,0,1:T(8,128)}, /*index=5*...) while((s32[]{:T(128)}, bf16[20,320,96]{1,2,0:T(8,128)(2,1)S(1)}, ...), condition=%wide.region_9.10_spmd, body=%wide.region_8.9_spmd.sunk | while | flops 478824032 | bytes 13565485 | solution.py:57
  10.9 22.0 %select_multiply_fusion.3 = (f32[320,1280]{1,0:T(8,128)S(1)}, f32[320,1280]{1,0:T(8,128)S(1)}) fusion(f32[]{:T(128)S(6)} %div.53, f32[]{:T(128)S(6)} %div.54, s32[]{:T(128)S(6)} %select_n.235, pred[1280]{0:T(1024)(128)(4,1)S(1)} %iota_compare_fusion.5, pred[]{:T(512)S(6)} %lt.148, pred[320]{0:T(512)(128)(4,1)S(1)} %iota_compare_fusion.6), kind=kLoop, calls=%fused_computation.6.clone.1 | loop fusion | flops 6144000 | bytes 3278413 | tf_op jit(solution)/shard_map/while/body/eval_jaxpr/mul | solution.py:20
  43.8 22.0 %select_multiply_fusion.3 = (f32[320,1280]{1,0:T(8,128)S(1)}, f32[320,1280]{1,0:T(8,128)S(1)}) fusion(f32[]{:T(128)S(6)} %div.53, f32[]{:T(128)S(6)} %div.54, s32[]{:T(128)S(6)} %select_n.235, pred[1280]{0:T(1024)(128)(4,1)S(1)} %iota_compare_fusion.5, pred[]{:T(512)S(6)} %lt.148, pred[320]{0:T(512)(128)(4,1)S(1)} %iota_compare_fusion.6), kind=kLoop, calls=%fused_computation.6.clone.1 | loop fusion | flops 6144000 | bytes 3278413 | tf_op jit(solution)/shard_map/while/body/eval_jaxpr/mul | solution.py:20
  76.8 22.0 %select_multiply_fusion.3 = (f32[320,1280]{1,0:T(8,128)S(1)}, f32[320,1280]{1,0:T(8,128)S(1)}) fusion(f32[]{:T(128)S(6)} %div.53, f32[]{:T(128)S(6)} %div.54, s32[]{:T(128)S(6)} %select_n.235, pred[1280]{0:T(1024)(128)(4,1)S(1)} %iota_compare_fusion.5, pred[]{:T(512)S(6)} %lt.148, pred[320]{0:T(512)(128)(4,1)S(1)} %iota_compare_fusion.6), kind=kLoop, calls=%fused_computation.6.clone.1 | loop fusion | flops 6144000 | bytes 3278413 | tf_op jit(solution)/shard_map/while/body/eval_jaxpr/mul | solution.py:20
  109.7 22.0 %select_multiply_fusion.3 = (f32[320,1280]{1,0:T(8,128)S(1)}, f32[320,1280]{1,0:T(8,128)S(1)}) fusion(f32[]{:T(128)S(6)} %div.53, f32[]{:T(128)S(6)} %div.54, s32[]{:T(128)S(6)} %select_n.235, pred[1280]{0:T(1024)(128)(4,1)S(1)} %iota_compare_fusion.5, pred[]{:T(512)S(6)} %lt.148, pred[320]{0:T(512)(128)(4,1)S(1)} %iota_compare_fusion.6), kind=kLoop, calls=%fused_computation.6.clone.1 | loop fusion | flops 6144000 | bytes 3278413 | tf_op jit(solution)/shard_map/while/body/eval_jaxpr/mul | solution.py:20
  142.6 22.0 %select_multiply_fusion.3 = (f32[320,1280]{1,0:T(8,128)S(1)}, f32[320,1280]{1,0:T(8,128)S(1)}) fusion(f32[]{:T(128)S(6)} %div.53, f32[]{:T(128)S(6)} %div.54, s32[]{:T(128)S(6)} %select_n.235, pred[1280]{0:T(1024)(128)(4,1)S(1)} %iota_compare_fusion.5, pred[]{:T(512)S(6)} %lt.148, pred[320]{0:T(512)(128)(4,1)S(1)} %iota_compare_fusion.6), kind=kLoop, calls=%fused_computation.6.clone.1 | loop fusion | flops 6144000 | bytes 3278413 | tf_op jit(solution)/shard_map/while/body/eval_jaxpr/mul | solution.py:20
  175.6 22.0 %select_multiply_fusion.3 = (f32[320,1280]{1,0:T(8,128)S(1)}, f32[320,1280]{1,0:T(8,128)S(1)}) fusion(f32[]{:T(128)S(6)} %div.53, f32[]{:T(128)S(6)} %div.54, s32[]{:T(128)S(6)} %select_n.235, pred[1280]{0:T(1024)(128)(4,1)S(1)} %iota_compare_fusion.5, pred[]{:T(512)S(6)} %lt.148, pred[320]{0:T(512)(128)(4,1)S(1)} %iota_compare_fusion.6), kind=kLoop, calls=%fused_computation.6.clone.1 | loop fusion | flops 6144000 | bytes 3278413 | tf_op jit(solution)/shard_map/while/body/eval_jaxpr/mul | solution.py:20
  208.5 22.0 %select_multiply_fusion.3 = (f32[320,1280]{1,0:T(8,128)S(1)}, f32[320,1280]{1,0:T(8,128)S(1)}) fusion(f32[]{:T(128)S(6)} %div.53, f32[]{:T(128)S(6)} %div.54, s32[]{:T(128)S(6)} %select_n.235, pred[1280]{0:T(1024)(128)(4,1)S(1)} %iota_compare_fusion.5, pred[]{:T(512)S(6)} %lt.148, pred[320]{0:T(512)(128)(4,1)S(1)} %iota_compare_fusion.6), kind=kLoop, calls=%fused_computation.6.clone.1 | loop fusion | flops 6144000 | bytes 3278413 | tf_op jit(solution)/shard_map/while/body/eval_jaxpr/mul | solution.py:20
  241.4 22.0 %select_multiply_fusion.3 = (f32[320,1280]{1,0:T(8,128)S(1)}, f32[320,1280]{1,0:T(8,128)S(1)}) fusion(f32[]{:T(128)S(6)} %div.53, f32[]{:T(128)S(6)} %div.54, s32[]{:T(128)S(6)} %select_n.235, pred[1280]{0:T(1024)(128)(4,1)S(1)} %iota_compare_fusion.5, pred[]{:T(512)S(6)} %lt.148, pred[320]{0:T(512)(128)(4,1)S(1)} %iota_compare_fusion.6), kind=kLoop, calls=%fused_computation.6.clone.1 | loop fusion | flops 6144000 | bytes 3278413 | tf_op jit(solution)/shard_map/while/body/eval_jaxpr/mul | solution.py:20
  274.4 22.0 %select_multiply_fusion.3 = (f32[320,1280]{1,0:T(8,128)S(1)}, f32[320,1280]{1,0:T(8,128)S(1)}) fusion(f32[]{:T(128)S(6)} %div.53, f32[]{:T(128)S(6)} %div.54, s32[]{:T(128)S(6)} %select_n.235, pred[1280]{0:T(1024)(128)(4,1)S(1)} %iota_compare_fusion.5, pred[]{:T(512)S(6)} %lt.148, pred[320]{0:T(512)(128)(4,1)S(1)} %iota_compare_fusion.6), kind=kLoop, calls=%fused_computation.6.clone.1 | loop fusion | flops 6144000 | bytes 3278413 | tf_op jit(solution)/shard_map/while/body/eval_jaxpr/mul | solution.py:20
  307.3 22.0 %select_multiply_fusion.3 = (f32[320,1280]{1,0:T(8,128)S(1)}, f32[320,1280]{1,0:T(8,128)S(1)}) fusion(f32[]{:T(128)S(6)} %div.53, f32[]{:T(128)S(6)} %div.54, s32[]{:T(128)S(6)} %select_n.235, pred[1280]{0:T(1024)(128)(4,1)S(1)} %iota_compare_fusion.5, pred[]{:T(512)S(6)} %lt.148, pred[320]{0:T(512)(128)(4,1)S(1)} %iota_compare_fusion.6), kind=kLoop, calls=%fused_computation.6.clone.1 | loop fusion | flops 6144000 | bytes 3278413 | tf_op jit(solution)/shard_map/while/body/eval_jaxpr/mul | solution.py:20
  340.2 22.0 %select_multiply_fusion.3 = (f32[320,1280]{1,0:T(8,128)S(1)}, f32[320,1280]{1,0:T(8,128)S(1)}) fusion(f32[]{:T(128)S(6)} %div.53, f32[]{:T(128)S(6)} %div.54, s32[]{:T(128)S(6)} %select_n.235, pred[1280]{0:T(1024)(128)(4,1)S(1)} %iota_compare_fusion.5, pred[]{:T(512)S(6)} %lt.148, pred[320]{0:T(512)(128)(4,1)S(1)} %iota_compare_fusion.6), kind=kLoop, calls=%fused_computation.6.clone.1 | loop fusion | flops 6144000 | bytes 3278413 | tf_op jit(solution)/shard_map/while/body/eval_jaxpr/mul | solution.py:20
  373.2 22.0 %select_multiply_fusion.3 = (f32[320,1280]{1,0:T(8,128)S(1)}, f32[320,1280]{1,0:T(8,128)S(1)}) fusion(f32[]{:T(128)S(6)} %div.53, f32[]{:T(128)S(6)} %div.54, s32[]{:T(128)S(6)} %select_n.235, pred[1280]{0:T(1024)(128)(4,1)S(1)} %iota_compare_fusion.5, pred[]{:T(512)S(6)} %lt.148, pred[320]{0:T(512)(128)(4,1)S(1)} %iota_compare_fusion.6), kind=kLoop, calls=%fused_computation.6.clone.1 | loop fusion | flops 6144000 | bytes 3278413 | tf_op jit(solution)/shard_map/while/body/eval_jaxpr/mul | solution.py:20
  406.1 22.0 %select_multiply_fusion.3 = (f32[320,1280]{1,0:T(8,128)S(1)}, f32[320,1280]{1,0:T(8,128)S(1)}) fusion(f32[]{:T(128)S(6)} %div.53, f32[]{:T(128)S(6)} %div.54, s32[]{:T(128)S(6)} %select_n.235, pred[1280]{0:T(1024)(128)(4,1)S(1)} %iota_compare_fusion.5, pred[]{:T(512)S(6)} %lt.148, pred[320]{0:T(512)(128)(4,1)S(1)} %iota_compare_fusion.6), kind=kLoop, calls=%fused_computation.6.clone.1 | loop fusion | flops 6144000 | bytes 3278413 | tf_op jit(solution)/shard_map/while/body/eval_jaxpr/mul | solution.py:20
  439.1 22.0 %select_multiply_fusion.3 = (f32[320,1280]{1,0:T(8,128)S(1)}, f32[320,1280]{1,0:T(8,128)S(1)}) fusion(f32[]{:T(128)S(6)} %div.53, f32[]{:T(128)S(6)} %div.54, s32[]{:T(128)S(6)} %select_n.235, pred[1280]{0:T(1024)(128)(4,1)S(1)} %iota_compare_fusion.5, pred[]{:T(512)S(6)} %lt.148, pred[320]{0:T(512)(128)(4,1)S(1)} %iota_compare_fusion.6), kind=kLoop, calls=%fused_computation.6.clone.1 | loop fusion | flops 6144000 | bytes 3278413 | tf_op jit(solution)/shard_map/while/body/eval_jaxpr/mul | solution.py:20
  472.0 22.0 %select_multiply_fusion.3 = (f32[320,1280]{1,0:T(8,128)S(1)}, f32[320,1280]{1,0:T(8,128)S(1)}) fusion(f32[]{:T(128)S(6)} %div.53, f32[]{:T(128)S(6)} %div.54, s32[]{:T(128)S(6)} %select_n.235, pred[1280]{0:T(1024)(128)(4,1)S(1)} %iota_compare_fusion.5, pred[]{:T(512)S(6)} %lt.148, pred[320]{0:T(512)(128)(4,1)S(1)} %iota_compare_fusion.6), kind=kLoop, calls=%fused_computation.6.clone.1 | loop fusion | flops 6144000 | bytes 3278413 | tf_op jit(solution)/shard_map/while/body/eval_jaxpr/mul | solution.py:20
  504.9 22.0 %select_multiply_fusion.3 = (f32[320,1280]{1,0:T(8,128)S(1)}, f32[320,1280]{1,0:T(8,128)S(1)}) fusion(f32[]{:T(128)S(6)} %div.53, f32[]{:T(128)S(6)} %div.54, s32[]{:T(128)S(6)} %select_n.235, pred[1280]{0:T(1024)(128)(4,1)S(1)} %iota_compare_fusion.5, pred[]{:T(512)S(6)} %lt.148, pred[320]{0:T(512)(128)(4,1)S(1)} %iota_compare_fusion.6), kind=kLoop, calls=%fused_computation.6.clone.1 | loop fusion | flops 6144000 | bytes 3278413 | tf_op jit(solution)/shard_map/while/body/eval_jaxpr/mul | solution.py:20
  537.9 22.0 %select_multiply_fusion.3 = (f32[320,1280]{1,0:T(8,128)S(1)}, f32[320,1280]{1,0:T(8,128)S(1)}) fusion(f32[]{:T(128)S(6)} %div.53, f32[]{:T(128)S(6)} %div.54, s32[]{:T(128)S(6)} %select_n.235, pred[1280]{0:T(1024)(128)(4,1)S(1)} %iota_compare_fusion.5, pred[]{:T(512)S(6)} %lt.148, pred[320]{0:T(512)(128)(4,1)S(1)} %iota_compare_fusion.6), kind=kLoop, calls=%fused_computation.6.clone.1 | loop fusion | flops 6144000 | bytes 3278413 | tf_op jit(solution)/shard_map/while/body/eval_jaxpr/mul | solution.py:20
  570.8 22.0 %select_multiply_fusion.3 = (f32[320,1280]{1,0:T(8,128)S(1)}, f32[320,1280]{1,0:T(8,128)S(1)}) fusion(f32[]{:T(128)S(6)} %div.53, f32[]{:T(128)S(6)} %div.54, s32[]{:T(128)S(6)} %select_n.235, pred[1280]{0:T(1024)(128)(4,1)S(1)} %iota_compare_fusion.5, pred[]{:T(512)S(6)} %lt.148, pred[320]{0:T(512)(128)(4,1)S(1)} %iota_compare_fusion.6), kind=kLoop, calls=%fused_computation.6.clone.1 | loop fusion | flops 6144000 | bytes 3278413 | tf_op jit(solution)/shard_map/while/body/eval_jaxpr/mul | solution.py:20
  603.7 22.0 %select_multiply_fusion.3 = (f32[320,1280]{1,0:T(8,128)S(1)}, f32[320,1280]{1,0:T(8,128)S(1)}) fusion(f32[]{:T(128)S(6)} %div.53, f32[]{:T(128)S(6)} %div.54, s32[]{:T(128)S(6)} %select_n.235, pred[1280]{0:T(1024)(128)(4,1)S(1)} %iota_compare_fusion.5, pred[]{:T(512)S(6)} %lt.148, pred[320]{0:T(512)(128)(4,1)S(1)} %iota_compare_fusion.6), kind=kLoop, calls=%fused_computation.6.clone.1 | loop fusion | flops 6144000 | bytes 3278413 | tf_op jit(solution)/shard_map/while/body/eval_jaxpr/mul | solution.py:20
  636.7 22.0 %select_multiply_fusion.3 = (f32[320,1280]{1,0:T(8,128)S(1)}, f32[320,1280]{1,0:T(8,128)S(1)}) fusion(f32[]{:T(128)S(6)} %div.53, f32[]{:T(128)S(6)} %div.54, s32[]{:T(128)S(6)} %select_n.235, pred[1280]{0:T(1024)(128)(4,1)S(1)} %iota_compare_fusion.5, pred[]{:T(512)S(6)} %lt.148, pred[320]{0:T(512)(128)(4,1)S(1)} %iota_compare_fusion.6), kind=kLoop, calls=%fused_computation.6.clone.1 | loop fusion | flops 6144000 | bytes 3278413 | tf_op jit(solution)/shard_map/while/body/eval_jaxpr/mul | solution.py:20
  704.3 23.8 %gather_fusion.2 = bf16[640,20,320]{2,1,0:T(8,128)(2,1)} fusion(bf16[20,320,320]{1,0,2:T(8,128)(2,1)} %copy.13, s32[1024]{0:T(1024)S(1)} %pad_clamp_fusion), kind=kCustom, calls=%fused_computation.2 | custom fusion | bytes 16386560 | tf_op jit(solution)/shard_map/jit(_take)/gather | solution.py:76
  740.1 21.7 %all-to-all-done = bf16[32,20,1920]{2,1,0:T(8,128)(2,1)S(1)} async-done(((bf16[32,20,1920]{2,1,0:T(8,128)(2,1)}), bf16[32,20,1920]{2,1,0:T(8,128)(2,1)S(1)}, u32[]{:S(2)}, u32[]{:S(2)}) %all-to-all-start) | async-done | bytes 2457632 | tf_op jit(solution)/shard_map/all_to_all | solution.py:72
  778.5 139.7 %psum.7 = f32[48,320]{1,0:T(8,128)S(1)} all-reduce(f32[48,320]{1,0:T(8,128)S(1)} %bitcast.58), channel_id=1, replica_groups=mesh['member'=8,'band'=32] {'band'}, use_global_device_ids=true, to_apply=%region_11.12 | all-reduce | flops 15360 | bytes 122880 | tf_op jit(solution)/shard_map/psum | solution.py:86
  (203 shorter events, 189.5 us)
Async XLA Ops:
  0.6 3.0 copy-start
  2.4 0.7 copy-start.4
  2.4 1.2 copy-start.3
  682.2 79.6 %all-to-all-start = ((bf16[32,20,1920]{2,1,0:T(8,128)(2,1)}), bf16[32,20,1920]{2,1,0:T(8,128)(2,1)S(1)}, u32[]{:S(2)}, u32[]{:S(2)}) async-start(bf16[32,20,1920]{2,1,0:T(8,128)(2,1)} %select_select_fusion), calls=%async_computation | async-start | bytes 5898240 | tf_op jit(solution)/shard_map/all_to_all | solution.py:72
  776.5 1.9 copy-start.2
  776.5 142.3 %copy-start.1 = (s32[640]{0:T(1024)S(1)}, s32[640]{0:T(1024)}, u32[]{:S(2)}) copy-start(s32[640]{0:T(1024)} %param.8) | copy-start | bytes 7684
where the time goes:
time: 922 us; the launch traced here: 919 us
  other arithmetic  476 us (52%)
  blocking collectives  140 us (15%)
  loops' own time  103 us (11%)
  matrix products  92.3 us (10%)
  local copies, waits for them, and re-layouts  73.9 us (8%)
  waiting for transfers between devices  21.7 us (2%)
  starting transfers between devices  11.5 us (1%)
    mul x20, other arithmetic, fourier_row(): jnp.cos(angle) * weight  440 us
    psum x1, blocking collectives, on_device(): power = lax.psum(local_power, 'band')  140 us
    another operation x1, loops' own time, on_device(): lax.map(transform_row, jnp.arange(row_count, dtype=jnp.int32))  103 us
    dot_general x20, matrix products, fourier_row(): lax.dot_general(table, row_values, (((1,), (1,)), ((), ())), precision=la...  83.2 us
    gather x1, local copies, waits for them, and re-layouts, on_device(): gathered = jnp.take(legendre, column, axis=2)  23.8 us
    all_to_all x1, waiting for transfers between devices, on_device(): lax.all_to_all(packed, 'band', split_axis=0, concat_axis=1, tiled=True)  21.7 us
  transfers between devices with their start and end apart: 1, of which 1 were waited for; matrix products, arithmetic and copies ran while one was open for 5% of the time, Pallas kernels for 0%

commit v1 on v0

v1 whole, which is shorter than its diff:
```python
import functools
import math

import jax
import jax.numpy as jnp
from jax import lax
from jax.experimental import pallas as pl
from jax.experimental.pallas import tpu as pltpu
from jax.sharding import PartitionSpec as P

NN = 320
F = 48
ROWS = 20
CAP = 20
BAND = 32
NLATH = 320
GROUPS = 4
LT = 248
VMEM = 56 * 1024 * 1024
MESH = pl.DeviceIdType.MESH


def cos_sin(turns):
    x = (turns - jnp.floor(turns + 0.5)) * (2.0 * math.pi)
    y = x * x
    c = jnp.full_like(x, 1.0 / math.factorial(20))
    for n in range(18, -2, -2):
        c = 1.0 / math.factorial(n) - c * y
    s = jnp.full_like(x, 1.0 / math.factorial(21))
    for n in range(19, -1, -2):
        s = 1.0 / math.factorial(n) - s * y
    return c, s * x


def cmul(a, b):
    return a[0] * b[0] - a[1] * b[1], a[0] * b[1] + a[1] * b[0]


def split(x):
    hi = x.astype(jnp.bfloat16)
    return hi, (x - hi.astype(jnp.float32)).astype(jnp.bfloat16)


def fourier_kernel(start_ref, lat_ref, points_ref, x_ref, out_ref, w_ref, bhi_ref, blo_ref, f_ref):
    r = pl.program_id(0)
    me = lax.axis_index("band")
    length = points_ref[lat_ref[me * ROWS + r]]
    quarter = length // 4
    f32 = jnp.float32

    @pl.when(r == 0)
    def _():
        f_ref[240 * 24 :, :] = jnp.zeros((8 * 24, 128), f32)
        zero = jnp.zeros((F, 384), jnp.bfloat16)
        for ref in (bhi_ref, blo_ref):
            ref[0:48, 384:768] = zero
            ref[48:96, 0:384] = zero

    qf = jnp.full((8, 128), quarter, jnp.int32).astype(f32)
    inv_q = 1.0 / qf
    inv_l = 0.25 * inv_q
    sub = lax.broadcasted_iota(jnp.int32, (8, 128), 0)
    lane = lax.broadcasted_iota(jnp.int32, (8, 128), 1)

    def turns_of(count):
        num = count.astype(f32)
        return (num - jnp.floor(num * inv_q) * qf) * inv_q

    table = cos_sin(turns_of(sub * lane))
    step = cos_sin(turns_of(8 * lane))
    tiles = [table]
    while len(tiles) < 48:
        room = 48 - len(tiles)
        tiles = tiles + [cmul(t, step) for t in tiles[:room]]
        step = cmul(step, step)
    for a in range(0, 48, 2):
        rows = 8 * a + lax.broadcasted_iota(jnp.int32, (16, 128), 0)
        scale = jnp.where(rows < quarter, jnp.concatenate([inv_l, inv_l], axis=0), 0.0)
        for part in range(2):
            value = jnp.concatenate([tiles[a][part], tiles[a + 1][part]], axis=0) * scale
            hi, lo = split(value)
            at = part * 384 + 8 * a
            w_ref[at : at + 16, 0:128] = hi
            w_ref[at : at + 16, 128:256] = lo

    psub = lax.broadcasted_iota(jnp.int32, (8, 384), 0)
    plane = lax.broadcasted_iota(jnp.int32, (8, 384), 1)
    lf = jnp.full((8, 384), length, jnp.int32).astype(f32)
    tc, ts = cos_sin((psub * plane).astype(f32) / lf)

    lane48 = lax.broadcasted_iota(jnp.int32, (F, 128), 1)

    def window(q):
        offset = q * quarter
        tile = offset >> 7
        rest = offset & 127
        parts = []
        for b in range(4):
            at = pl.multiple_of(jnp.minimum(tile + b, 9) * 128, 128)
            parts.append(pltpu.roll(x_ref[0, :, pl.ds(at, 128)], (128 - rest) & 127, axis=1))
        here = lane48 < 128 - rest
        return [jnp.where(here, parts[b], parts[b + 1]) for b in range(3)]

    w1, w2, w3 = window(1), window(2), window(3)
    for b in range(3):
        lo_at, hi_at = 128 * b, 128 * b + 128
        x0 = x_ref[0, :, lo_at:hi_at]
        e0, o0 = x0 + w2[b], x0 - w2[b]
        e1, o1 = w1[b] + w3[b], w1[b] - w3[b]
        c1, c2, c3 = (tc[p : p + 1, lo_at:hi_at] for p in (1, 2, 3))
        s1, s2, s3 = (ts[p : p + 1, lo_at:hi_at] for p in (1, 2, 3))
        y2 = e0 - e1
        pairs = [
            (e0 + e1, None),
            (o0 * c1 - o1 * s1, -(o0 * s1 + o1 * c1)),
            (y2 * c2, -(y2 * s2)),
            (o0 * c3 + o1 * s3, o1 * c3 - o0 * s3),
        ]
        for p, (zr, zi) in enumerate(pairs):
            top, mid = 96 * p, 96 * p + 48
            for ref, value in zip((bhi_ref, blo_ref), split(zr)):
                ref[top : top + 48, lo_at:hi_at] = value
                ref[mid : mid + 48, 384 + lo_at : 384 + hi_at] = -value
            if zi is not None:
                for ref, value in zip((bhi_ref, blo_ref), split(zi)):
                    ref[top : top + 48, 384 + lo_at : 384 + hi_at] = value
                    ref[mid : mid + 48, lo_at:hi_at] = value

    first = jnp.dot(bhi_ref[...], w_ref[...], preferred_element_type=f32)
    second = jnp.dot(blo_ref[...], w_ref[:, 0:128], preferred_element_type=f32)
    total = first[:, 0:128] + first[:, 128:256] + second
    for t in range(3):
        turned = total[128 * t : 128 * t + 128].T[:80]
        k = lax.broadcasted_iota(jnp.int32, (80, 128), 0)
        col = 128 * t + lax.broadcasted_iota(jnp.int32, (80, 128), 1)
        p = (col >= 96).astype(jnp.int32) + (col >= 192).astype(jnp.int32) + (col >= 288).astype(jnp.int32)
        kept = jnp.where(4 * k + p < length // 2, turned, 0.0)
        f_ref[pl.ds(t * 24 + r, 80, stride=72), :] = kept

    @pl.when(r == ROWS - 1)
    def _():
        lane24 = lax.broadcasted_iota(jnp.int32, (24, 128), 1)
        low = lax.broadcasted_iota(jnp.int32, (8, 128), 0) < 4

        def pack(d, carry):
            for g in range(GROUPS):
                order = jnp.minimum(start_ref[d] + 5 * g, NN)
                at = pl.multiple_of(((3 * order) >> 2) * 24, 8)
                rest = (96 * order) & 127
                rolled = pltpu.roll(f_ref[pl.ds(at, 120), :], (128 - rest) & 127, axis=1)
                here = lane24 < 128 - rest
                tails = []
                for j in range(4):
                    v = jnp.where(here, rolled[24 * j : 24 * j + 24], rolled[24 * j + 24 : 24 * j + 48])
                    out_ref[g, d, 16 * j : 16 * j + 16, :] = v[:16].astype(jnp.bfloat16)
                    tails.append(v[16:24])
                ext = jnp.concatenate(
                    [jnp.where(low, tails[j], pltpu.roll(tails[j + 1], 4, axis=0)) for j in (0, 2)], axis=0
                )
                out_ref[g, d, 64:80, :] = ext.astype(jnp.bfloat16)
            return carry

        lax.fori_loop(0, BAND, pack, 0)


def fourier(starts, row_latitude, row_points, rows):
    smem = pl.BlockSpec(memory_space=pltpu.SMEM)
    return pl.pallas_call(
        fourier_kernel,
        grid=(ROWS,),
        in_specs=[smem, smem, smem, pl.BlockSpec((1, F, 1280), lambda r: (r, 0, 0))],
        out_specs=pl.BlockSpec((GROUPS, BAND, 80, 128), lambda r: (0, 0, 0, 0)),
        out_shape=jax.ShapeDtypeStruct((GROUPS, BAND, 80, 128), jnp.bfloat16),
        scratch_shapes=[
            pltpu.VMEM((768, 256), jnp.bfloat16),
            pltpu.VMEM((384, 768), jnp.bfloat16),
            pltpu.VMEM((384, 768), jnp.bfloat16),
            pltpu.VMEM((LT * 24, 128), jnp.float32),
        ],
        compiler_params=pltpu.CompilerParams(vmem_limit_bytes=VMEM),
        name="fourier",
    )(starts, row_latitude, row_points, rows)


def exchange_kernel(start_ref, send_ref, leg_ref, pick_ref, spec_ref, energy_ref,
                    recv, lp, xt, power, pieces, parts, result, final,
                    send_sem, recv_sem, own_sem, power_send, power_recv, final_send, final_recv):
    me = lax.axis_index("band")
    f32 = jnp.float32
    barrier = pltpu.get_barrier_semaphore()

    def greet(o, carry):
        pl.semaphore_signal(barrier, inc=1, device_id={"band": lax.rem(me + o, BAND)}, device_id_type=MESH)
        return carry

    lax.fori_loop(1, BAND, greet, 0)
    own = [pltpu.make_async_copy(send_ref.at[g, me], recv.at[g, me], own_sem.at[g]) for g in range(GROUPS)]
    for copy in own:
        copy.start()
    pl.semaphore_wait(barrier, BAND - 1)

    for g in range(GROUPS):
        def send(o, carry, g=g):
            peer = lax.rem(me + o, BAND)
            pltpu.make_async_remote_copy(
                src_ref=send_ref.at[g, peer],
                dst_ref=recv.at[g, me],
                send_sem=send_sem.at[g],
                recv_sem=recv_sem.at[g],
                device_id={"band": peer},
                device_id_type=MESH,
            ).start()
            return carry

        lax.fori_loop(1, BAND, send, 0)

    start = start_ref[me]
    count = start_ref[me + 1] - start
    degree = lax.broadcasted_iota(jnp.int32, (1, NN), 1)

    def permute(s, carry):
        sign = (1 - 2 * ((degree + start + s) & 1)).astype(f32)
        value = lax.dot_general(
            pick_ref[...], leg_ref[s], (((1,), (1,)), ((), ())), preferred_element_type=f32
        )
        lp[s, 0:256, :] = value[0:256].astype(jnp.bfloat16)
        lp[s, 256:512, :] = (value[256:512] * sign).astype(jnp.bfloat16)
        lp[s, 512:576, :] = value[512:576].astype(jnp.bfloat16)
        lp[s, 576:640, :] = (value[576:640] * sign).astype(jnp.bfloat16)
        return carry

    lax.fori_loop(0, CAP, permute, 0)
    power[...] = jnp.zeros_like(power)
    low = lax.broadcasted_iota(jnp.int32, (16, 8, 128), 1) < 4

    for g in range(GROUPS):
        own[g].wait()
        everyone = recv.at[g, 0 : BAND - 1]
        pltpu.make_async_copy(everyone, everyone, recv_sem.at[g]).wait()
        tails = recv[g, :, 64:80, :].astype(f32).reshape(16, 2, 2, 8, 128)
        for a in range(4):
            main = recv[g, :, 16 * a : 16 * a + 16, :].reshape(512, 128)
            xt[128 * a : 128 * a + 128, 0:512] = main.T
            even, odd = tails[:, 0, a // 2], tails[:, 1, a // 2]
            if a % 2 == 0:
                tail = jnp.where(low, even, pltpu.roll(odd, 4, axis=1))
            else:
                tail = jnp.where(low, pltpu.roll(even, 4, axis=1), odd)
            xt[128 * a : 128 * a + 128, 512:640] = tail.reshape(128, 128).T.astype(jnp.bfloat16)
        for i in range(5):
            s = 5 * g + i
            order = start + s
            value = jnp.dot(xt[96 * i : 96 * i + 96, :], lp[s], preferred_element_type=f32)
            first = jnp.where(s < count, order, NN)
            value = jnp.where(degree >= first, value, 0.0)
            spec_ref[s] = value
            weight = jnp.where(order == 0, 1.0, 2.0).astype(f32)
            re, im = value[0:48], value[48:96]
            power[:, 0:NN] += weight * (re * re + im * im)

    for j in range(18):
        pieces[j] = power[8 * (j // 3) : 8 * (j // 3) + 8, 128 * (j % 3) : 128 * (j % 3) + 128]

    def spread(j, carry):
        @pl.when(j != me)
        def _():
            pltpu.make_async_remote_copy(
                src_ref=pieces.at[j], dst_ref=parts.at[me], send_sem=power_send, recv_sem=power_recv,
                device_id={"band": j}, device_id_type=MESH,
            ).start()
        return carry

    lax.fori_loop(0, 18, spread, 0)

    @pl.when(me < 18)
    def _():
        parts[me] = pieces[me]
        others = parts.at[0 : BAND - 1]
        pltpu.make_async_copy(others, others, power_recv).wait()
        column = 128 * lax.rem(me, 3) + lax.broadcasted_iota(jnp.int32, (8, 128), 1)
        value = jnp.sum(parts[...], axis=0) / (2 * column + 1).astype(f32)
        result[...] = value
        final[me] = value

        def share(o, carry):
            pltpu.make_async_remote_copy(
                src_ref=result, dst_ref=final.at[me], send_sem=final_send, recv_sem=final_recv,
                device_id={"band": lax.rem(me + o, BAND)}, device_id_type=MESH,
            ).start()
            return carry

        lax.fori_loop(1, BAND, share, 0)
        most = final.at[0:17]
        pltpu.make_async_copy(most, most, final_recv).wait()
        pltpu.make_async_copy(others, others, final_send).wait()
        sent = pieces.at[0:17]
        pltpu.make_async_copy(sent, sent, power_send).wait()

    @pl.when(me >= 18)
    def _():
        pltpu.make_async_copy(final, final, final_recv).wait()
        pltpu.make_async_copy(pieces, pieces, power_send).wait()

    for j in range(18):
        g, t = j // 3, j % 3
        width = 128 if t < 2 else 64
        energy_ref[8 * g : 8 * g + 8, 128 * t : 128 * t + width] = final[j][:, :width]

    for g in range(GROUPS):
        everyone = send_ref.at[g, 0 : BAND - 1]
        pltpu.make_async_copy(everyone, everyone, send_sem.at[g]).wait()


def exchange(starts, packed, legendre, pick):
    vmem = pl.BlockSpec(memory_space=pltpu.VMEM)
    return pl.pallas_call(
        exchange_kernel,
        in_specs=[pl.BlockSpec(memory_space=pltpu.SMEM), pl.BlockSpec(memory_space=pl.ANY), vmem, vmem],
        out_specs=[vmem, vmem],
        out_shape=[
            jax.ShapeDtypeStruct((CAP, 2 * F, NN), jnp.float32),
            jax.ShapeDtypeStruct((F, NN), jnp.float32),
        ],
        scratch_shapes=[
            pltpu.VMEM((GROUPS, BAND, 80, 128), jnp.bfloat16),
            pltpu.VMEM((CAP, 640, NN), jnp.bfloat16),
            pltpu.VMEM((512, 640), jnp.bfloat16),
            pltpu.VMEM((F, 384), jnp.float32),
            pltpu.VMEM((18, 8, 128), jnp.float32),
            pltpu.VMEM((BAND, 8, 128), jnp.float32),
            pltpu.VMEM((8, 128), jnp.float32),
            pltpu.VMEM((18, 8, 128), jnp.float32),
            pltpu.SemaphoreType.DMA((GROUPS,)),
            pltpu.SemaphoreType.DMA((GROUPS,)),
            pltpu.SemaphoreType.DMA((GROUPS,)),
            pltpu.SemaphoreType.DMA,
            pltpu.SemaphoreType.DMA,
            pltpu.SemaphoreType.DMA,
            pltpu.SemaphoreType.DMA,
        ],
        compiler_params=pltpu.CompilerParams(collective_id=0, has_side_effects=True, vmem_limit_bytes=VMEM),
        name="exchange",
    )(starts, packed, legendre, pick)


def on_device(grid, row_points, row_latitude, order_owner, legendre):
    bands = jnp.arange(BAND + 1, dtype=jnp.int32)
    starts = jnp.sum((order_owner[None, :] < bands[:, None]).astype(jnp.int32), axis=1)
    by_device = row_latitude.reshape(BAND, ROWS)
    stacked = jnp.concatenate([by_device[:, :16].reshape(-1), by_device[:, 16:].reshape(-1)])
    column = jnp.where(stacked < NLATH, stacked, 2 * NLATH - 1 - stacked)
    pick = (column[:, None] == jnp.arange(NLATH, dtype=jnp.int32)[None, :]).astype(jnp.bfloat16)
    packed = fourier(starts, row_latitude, row_points, jnp.transpose(grid, (1, 0, 2)))
    spectral, energy = exchange(starts, packed, legendre, pick)
    return spectral.reshape(CAP, 2, F, NN), energy


def solution(mesh):
    in_specs = (P("member", "band", None), P(), P(), P(), P("band", None, None))
    out_specs = (P("band", None, "member", None), P("member", None))
    return jax.shard_map(
        on_device, mesh=mesh, in_specs=in_specs, out_specs=out_specs, check_vma=False
    )
```

time: 922 us -> 119 us (0.13)
  other arithmetic: 476 us -> 2.27 us
  blocking collectives: 140 us -> 0 us
  Pallas kernels: 0 us -> 110 us
  loops' own time: 103 us -> 0 us
  matrix products: 92.3 us -> 0 us
  local copies, waits for them, and re-layouts: 73.9 us -> 5.36 us
  waiting for transfers between devices: 21.7 us -> 0 us
  starting transfers between devices: 11.5 us -> 0 us
    mul x20 -> x0, other arithmetic: 440 us -> none  [fourier_row(): jnp.cos(angle) * weight]
    psum x1 -> x0, blocking collectives: 140 us -> none  [on_device(): power = lax.psum(local_power, 'band')]
    pallas_call x0 -> x2, Pallas kernels: none -> 110 us  [the longest x1 86.8 us: exchange(): pl.pallas_call(exchange_kernel, in_specs=[pl.BlockSpec(memory_space=pltpu...]
    another operation x1 -> x0, loops' own time: 103 us -> none  [on_device(): lax.map(transform_row, jnp.arange(row_count, dtype=jnp.int32))]
    dot_general x22 -> x0, matrix products: 92.3 us -> none  [the longest x20 83.2 us: fourier_row(): lax.dot_general(table, row_values, (((1,), (1,)), ((), ())), precision=la...]
    gather x4 -> x0, local copies, waits for them, and re-layouts: 31.1 us -> none  [the longest x1 23.8 us: on_device(): gathered = jnp.take(legendre, column, axis=2)]
    dynamic_slice x40 -> x0, local copies, waits for them, and re-layouts: 23.5 us -> none  [the longest x20 11.7 us: on_device(): lax.map(transform_row, jnp.arange(row_count, dtype=jnp.int32))]
    all_to_all x1 -> x0, waiting for transfers between devices: 21.7 us -> none  [on_device(): lax.all_to_all(packed, 'band', split_axis=0, concat_axis=1, tiled=True)]
  transfers between devices with their start and end apart: 1 -> 0, of which waited for: 1 -> 0; matrix products, arithmetic and copies ran while one was open for 5% -> 0% of each run, Pallas kernels for 0% -> 0%
where the time goes in v1:
time: 119 us
  Pallas kernels  110 us (92%)
  local copies, waits for them, and re-layouts  5.36 us (5%)
  other arithmetic  2.27 us (2%)
    pallas_call x1, Pallas kernels, exchange(): pl.pallas_call(exchange_kernel, in_specs=[pl.BlockSpec(memory_space=pltpu...  86.8 us
    pallas_call x1, Pallas kernels, fourier(): pl.pallas_call(fourier_kernel, grid=(ROWS,), in_specs=[smem, smem, smem,...  23.6 us
    unnamed x5, local copies, waits for them, and re-layouts  4.31 us

profile of v1, /device:TPU:2, one launch (start us, length us, event | category | flops | bytes accessed | tf_op | source)
XLA Modules:
  0.0 118.7 jit_solution(14492284655281145602)
XLA Ops:
  0.6 1.3 %convert_reduce_fusion.start_ref = s32[33]{0:T(128)} fusion(s32[320]{0:T(512)} %param.8), kind=kLoop, calls=%fused_computation.2 | loop fusion | flops 31647 | bytes 1412 | tf_op jit(solution)/shard_map/reduce_sum | solution.py:348
  1.9 0.8 reshape.56
  2.7 0.1 concatenate.17
  2.8 0.1 slice.9
  2.9 0.1 concatenate.18
  3.0 0.9 fusion.pick_ref
  4.0 23.6 %fourier.1.send_ref = bf16[4,32,80,128]{3,2,1,0:T(8,128)(2,1)} custom-call(s32[33]{0:T(128)} %convert_reduce_fusion.start_ref, s32[640]{0:T(1024)} %lat_ref.1, s32[640]{0:T(1024)} %points_ref.1, f32[20,48,1280]{2,1,0:T(8,128)} %bitcast.3), custom_call_target="tpu_custom_call" | custom-call | tf_op jit(solution)/shard_map/fourier/pallas_call | solution.py:168
  27.6 86.8 %exchange.1 = (f32[20,96,320]{2,1,0:T(8,128)}, f32[48,320]{1,0:T(8,128)}) custom-call(s32[33]{0:T(128)} %convert_reduce_fusion.start_ref, bf16[4,32,80,128]{3,2,1,0:T(8,128)(2,1)} %fourier.1.send_ref, bf16[20,320,320]{2,1,0:T(8,128)(2,1)} %leg_ref.1, bf16[640,320]{1,0:T(8,128)(2,1)} %fusion.pick_ref), custom_call_target="tpu_custom_call" | custom-call | tf_op jit(solution)/shard_map/exchange/pallas_call | solution.py:316
  114.4 0.0 copy-start
  114.4 3.7 %copy.11 = f32[20,2,48,320]{3,2,1,0:T(8,128)} copy(f32[20,2,48,320]{3,2,1,0:T(8,128)} %bitcast.4) | data formatting | bytes 4915200
  118.1 0.0 copy-done
  118.1 0.6 copy.12
  (4 shorter events, 0.0 us)
Async XLA Ops:
  114.4 3.7 %copy-start = (f32[48,320]{1,0:T(8,128)S(1)}, f32[48,320]{1,0:T(8,128)}, u32[]{:S(2)}) copy-start(f32[48,320]{1,0:T(8,128)} %get-tuple-element.9) | copy-start | bytes 184324

commit v2 on v1

v2 whole, which is shorter than its diff:
```python
import functools
import math

import jax
import jax.numpy as jnp
from jax import lax
from jax.experimental import pallas as pl
from jax.experimental.pallas import tpu as pltpu
from jax.sharding import PartitionSpec as P

NN = 320
F = 48
ROWS = 20
CAP = 20
BAND = 32
NLATH = 320
SHORT = 10
LT = 248
VMEM = 56 * 1024 * 1024
MESH = pl.DeviceIdType.MESH
F32 = jnp.float32
BF16 = jnp.bfloat16


def cos_sin(turns):
    x = (turns - jnp.floor(turns + 0.5)) * (2.0 * math.pi)
    y = x * x
    c = jnp.full_like(x, 1.0 / math.factorial(20))
    for n in range(18, -2, -2):
        c = 1.0 / math.factorial(n) - c * y
    s = jnp.full_like(x, 1.0 / math.factorial(21))
    for n in range(19, -1, -2):
        s = 1.0 / math.factorial(n) - s * y
    return c, s * x


def cmul(a, b):
    return a[0] * b[0] - a[1] * b[1], a[0] * b[1] + a[1] * b[0]


def split(x):
    hi = x.astype(BF16)
    return hi, (x - hi.astype(F32)).astype(BF16)


def dft_row(x_ref, tile_ref, r, length, w_ref, bhi_ref, blo_ref, f_ref, slot):
    quarter = length // 4
    for t in range(10):
        tile_ref[t] = x_ref[r, :, 128 * t : 128 * t + 128]

    qf = jnp.full((8, 128), quarter, jnp.int32).astype(F32)
    inv_q = 1.0 / qf
    inv_l = 0.25 * inv_q
    sub = lax.broadcasted_iota(jnp.int32, (8, 128), 0)
    lane = lax.broadcasted_iota(jnp.int32, (8, 128), 1)

    def turns_of(count):
        num = count.astype(F32)
        return (num - jnp.floor(num * inv_q) * qf) * inv_q

    step = cos_sin(turns_of(8 * lane))
    tiles = [cos_sin(turns_of(sub * lane))]
    while len(tiles) < 48:
        room = 48 - len(tiles)
        tiles = tiles + [cmul(t, step) for t in tiles[:room]]
        step = cmul(step, step)
    for a in range(0, 48, 2):
        rows = 8 * a + lax.broadcasted_iota(jnp.int32, (16, 128), 0)
        scale = jnp.where(rows < quarter, jnp.concatenate([inv_l, inv_l], axis=0), 0.0)
        for part in range(2):
            value = jnp.concatenate([tiles[a][part], tiles[a + 1][part]], axis=0) * scale
            hi, lo = split(value)
            at = part * 384 + 8 * a
            w_ref[at : at + 16, 0:128] = hi
            w_ref[at : at + 16, 128:256] = lo

    psub = lax.broadcasted_iota(jnp.int32, (8, 384), 0)
    plane = lax.broadcasted_iota(jnp.int32, (8, 384), 1)
    lf = jnp.full((8, 384), length, jnp.int32).astype(F32)
    tc, ts = cos_sin((psub * plane).astype(F32) / lf)

    lane48 = lax.broadcasted_iota(jnp.int32, (F, 128), 1)

    def window(q):
        offset = q * quarter
        tile = offset >> 7
        rest = offset & 127
        parts = []
        for b in range(4):
            parts.append(pltpu.roll(tile_ref[jnp.minimum(tile + b, 9)], (128 - rest) & 127, axis=1))
        here = lane48 < 128 - rest
        return [jnp.where(here, parts[b], parts[b + 1]) for b in range(3)]

    w1, w2, w3 = window(1), window(2), window(3)
    for b in range(3):
        lo_at, hi_at = 128 * b, 128 * b + 128
        x0 = x_ref[r, :, lo_at:hi_at]
        e0, o0 = x0 + w2[b], x0 - w2[b]
        e1, o1 = w1[b] + w3[b], w1[b] - w3[b]
        c1, c2, c3 = (tc[p : p + 1, lo_at:hi_at] for p in (1, 2, 3))
        s1, s2, s3 = (ts[p : p + 1, lo_at:hi_at] for p in (1, 2, 3))
        y2 = e0 - e1
        pairs = [
            (e0 + e1, None),
            (o0 * c1 - o1 * s1, -(o0 * s1 + o1 * c1)),
            (y2 * c2, -(y2 * s2)),
            (o0 * c3 + o1 * s3, o1 * c3 - o0 * s3),
        ]
        for p, (zr, zi) in enumerate(pairs):
            top, mid = 96 * p, 96 * p + 48
            for ref, value in zip((bhi_ref, blo_ref), split(zr)):
                ref[top : top + 48, lo_at:hi_at] = value
                ref[mid : mid + 48, 384 + lo_at : 384 + hi_at] = -value
            if zi is not None:
                for ref, value in zip((bhi_ref, blo_ref), split(zi)):
                    ref[top : top + 48, 384 + lo_at : 384 + hi_at] = value
                    ref[mid : mid + 48, lo_at:hi_at] = value

    first = jnp.dot(bhi_ref[...], w_ref[...], preferred_element_type=F32)
    second = jnp.dot(blo_ref[...], w_ref[:, 0:128], preferred_element_type=F32)
    total = first[:, 0:128] + first[:, 128:256] + second
    for t in range(3):
        turned = total[128 * t : 128 * t + 128].T[:80]
        k = lax.broadcasted_iota(jnp.int32, (80, 128), 0)
        col = 128 * t + lax.broadcasted_iota(jnp.int32, (80, 128), 1)
        p = sum((col >= 96 * q).astype(jnp.int32) for q in (1, 2, 3))
        kept = jnp.where(4 * k + p < length // 2, turned, 0.0)
        f_ref[pl.ds(t, 80, stride=3), slot, :] = kept


def take_orders(f_ref, order, height):
    order = jnp.minimum(order, NN)
    rest = (96 * order) & 127
    tiles = f_ref[pl.ds((3 * order) >> 2, 5)].reshape(5 * height, 128)
    rolled = pltpu.roll(tiles, (128 - rest) & 127, axis=1)
    here = lax.broadcasted_iota(jnp.int32, (height, 128), 1) < 128 - rest
    cut = [rolled[height * j : height * (j + 1)] for j in range(5)]
    return [jnp.where(here, cut[j], cut[j + 1]) for j in range(4)]


def pack_a(f_ref, order):
    return jnp.concatenate(take_orders(f_ref, order, 8), axis=0).astype(BF16)


def pack_b(f_ref, order):
    v = take_orders(f_ref, order, 16)
    low = lax.broadcasted_iota(jnp.int32, (8, 128), 0) < 4
    tails = [jnp.where(low, v[j][8:], pltpu.roll(v[j + 1][8:], 4, axis=0)) for j in (0, 2)]
    return jnp.concatenate([v[j][:8] for j in range(4)] + tails, axis=0).astype(BF16)


def octets(block):
    wide = block.astype(F32).reshape(BAND, 4, 8, 128)
    return [wide[:, a].reshape(256, 128).T.astype(BF16) for a in range(4)]


def quads(block):
    wide = block.astype(F32).reshape(16, 2, 2, 8, 128)
    low = lax.broadcasted_iota(jnp.int32, (16, 8, 128), 1) < 4
    out = []
    for a in range(4):
        even, odd = wide[:, 0, a // 2], wide[:, 1, a // 2]
        if a % 2 == 0:
            tail = jnp.where(low, even, pltpu.roll(odd, 4, axis=1))
        else:
            tail = jnp.where(low, pltpu.roll(even, 4, axis=1), odd)
        out.append(tail.reshape(128, 128).T.astype(BF16))
    return out


def wait(ref, sem):
    pltpu.make_async_copy(ref, ref, sem).wait()


def fused_kernel(short, start_ref, lat_ref, points_ref, grid_ref, leg_hbm, pick_ref, spec_ref, energy_ref,
                 x_ref, tile_ref, leg_ref, w_ref, bhi_ref, blo_ref, fa_ref, fb_ref,
                 send_a, send_b, recv_a, recv_b, over_a, over_b,
                 lp, xt, spec, power, pieces, parts, result, final,
                 x_sem, leg_sem, spec_sem, sent_a, sent_b, got_a, got_b,
                 hop1_sent, hop1_got, hop2_sent, hop2_got,
                 power_send, power_recv, final_send, final_recv):
    groups = 2 if short else 4
    me = lax.axis_index("band")
    z, y = me // 4, lax.rem(me, 4)
    barrier = pltpu.get_barrier_semaphore()

    def greet(o, carry):
        pl.semaphore_signal(barrier, inc=1, device_id={"band": lax.rem(me + o, BAND)}, device_id_type=MESH)
        return carry

    def load(r):
        return pltpu.make_async_copy(grid_ref.at[r], x_ref.at[r], x_sem.at[r])

    def load_row(r, carry):
        load(r).start()
        return carry

    lax.fori_loop(0, ROWS, load_row, 0)
    lax.fori_loop(1, BAND, greet, 0)
    leg_copy = pltpu.make_async_copy(leg_hbm, leg_ref, leg_sem)
    leg_copy.start()

    fa_ref[240:] = jnp.zeros((8, 8, 128), F32)
    fb_ref[240:] = jnp.zeros((8, 16, 128), F32)
    zero = jnp.zeros((F, 384), BF16)
    for ref in (bhi_ref, blo_ref):
        ref[0:48, 384:768] = zero
        ref[48:96, 0:384] = zero

    def dft(first, f_ref):
        def body(r, carry):
            load(r).wait()
            length = points_ref[lat_ref[me * ROWS + r]]
            dft_row(x_ref, tile_ref, r, length, w_ref, bhi_ref, blo_ref, f_ref, r - first)
            return carry
        return body

    def pack_all(packer, f_ref, send, recv, over):
        def body(d, carry):
            for g in range(groups):
                send[g, d] = packer(f_ref, start_ref[d] + 5 * g)
            return carry
        lax.fori_loop(0, BAND, body, 0)
        for g in range(groups):
            recv[g, me] = send[g, me]
        if short:
            for j in range(2):
                over[z, y, j] = packer(f_ref, start_ref[BAND + 1] + 5 * j)

    def send_all(c, send, recv, over, sent, got):
        if short:
            def hop1(o, carry):
                pltpu.make_async_remote_copy(
                    src_ref=over.at[z, y], dst_ref=over.at[z, y],
                    send_sem=hop1_sent.at[c], recv_sem=hop1_got.at[c],
                    device_id={"band": lax.rem(z + o, 8) * 4 + y}, device_id_type=MESH,
                ).start()
                return carry
            lax.fori_loop(1, 8, hop1, 0)
        for g in range(groups):
            def body(o, carry, g=g):
                peer = lax.rem(me + o, BAND)
                pltpu.make_async_remote_copy(
                    src_ref=send.at[g, peer], dst_ref=recv.at[g, me],
                    send_sem=sent.at[g], recv_sem=got.at[g],
                    device_id={"band": peer}, device_id_type=MESH,
                ).start()
                return carry
            lax.fori_loop(1, BAND, body, 0)

    def forward(c, over):
        wait(over.at[0:7, 0], hop1_got.at[c])
        def hop2(o, carry):
            pltpu.make_async_remote_copy(
                src_ref=over.at[:, y], dst_ref=over.at[:, y],
                send_sem=hop2_sent.at[c], recv_sem=hop2_got.at[c],
                device_id={"band": z * 4 + lax.rem(y + o, 4)}, device_id_type=MESH,
            ).start()
            return carry
        lax.fori_loop(1, 4, hop2, 0)

    lax.fori_loop(0, 8, dft(0, fa_ref), 0)
    pack_all(pack_a, fa_ref, send_a, recv_a, over_a)
    pl.semaphore_wait(barrier, BAND - 1)
    send_all(0, send_a, recv_a, over_a, sent_a, got_a)
    lax.fori_loop(8, ROWS, dft(8, fb_ref), 0)
    pack_all(pack_b, fb_ref, send_b, recv_b, over_b)
    send_all(1, send_b, recv_b, over_b, sent_b, got_b)
    leg_copy.wait()

    start = start_ref[me]
    count = start_ref[me + 1] - start
    degree = lax.broadcasted_iota(jnp.int32, (1, NN), 1)

    def permute(s, carry):
        sign = (1 - 2 * ((degree + start + s) & 1)).astype(F32)
        value = lax.dot_general(
            pick_ref[...], leg_ref[s], (((1,), (1,)), ((), ())), preferred_element_type=F32
        )
        for at, size, south in ((0, 128, 0), (128, 128, 1), (256, 128, 0), (384, 128, 1), (512, 64, 0), (576, 64, 1)):
            piece = value[at : at + size]
            lp[s, at : at + size, :] = (piece * sign if south else piece).astype(BF16)
        return carry

    lax.fori_loop(0, SHORT, permute, 0)
    if short:
        forward(0, over_a)
    lax.fori_loop(SHORT, CAP, permute, 0)
    if short:
        forward(1, over_b)
    power[...] = jnp.zeros_like(power)

    for g in range(4):
        if g < groups:
            wait(recv_a.at[g, 0 : BAND - 1], got_a.at[g])
            block_a = recv_a[g]
        else:
            if g == groups:
                wait(over_a.at[:, 0:3], hop2_got.at[0])
            block_a = over_a[:, :, g - groups].reshape(BAND, 32, 128)
        for a, value in enumerate(octets(block_a)):
            xt[128 * a : 128 * a + 128, 0:256] = value
        if g < groups:
            wait(recv_b.at[g, 0 : BAND - 1], got_b.at[g])
            block_b = recv_b[g]
        else:
            if g == groups:
                wait(over_b.at[:, 0:3], hop2_got.at[1])
            block_b = over_b[:, :, g - groups].reshape(BAND, 48, 128)
        for a, value in enumerate(octets(block_b[:, 0:32])):
            xt[128 * a : 128 * a + 128, 256:512] = value
        for a, value in enumerate(quads(block_b[:, 32:48])):
            xt[128 * a : 128 * a + 128, 512:640] = value
        for i in range(5):
            s = 5 * g + i
            order = start + s
            value = jnp.dot(xt[96 * i : 96 * i + 96, :], lp[s], preferred_element_type=F32)
            first = jnp.where(s < count, order, NN)
            value = jnp.where(degree >= first, value, 0.0)
            spec[s] = value
            weight = jnp.where(order == 0, 1.0, 2.0).astype(F32)
            re, im = value[0:48], value[48:96]
            power[:, 0:NN] += weight * (re * re + im * im)
        pltpu.make_async_copy(spec.at[5 * g : 5 * g + 5], spec_ref.at[5 * g : 5 * g + 5], spec_sem.at[g]).start()

    for j in range(18):
        pieces[j] = power[8 * (j // 3) : 8 * (j // 3) + 8, 128 * (j % 3) : 128 * (j % 3) + 128]

    def spread(j, carry):
        @pl.when(j != me)
        def _():
            pltpu.make_async_remote_copy(
                src_ref=pieces.at[j], dst_ref=parts.at[me], send_sem=power_send, recv_sem=power_recv,
                device_id={"band": j}, device_id_type=MESH,
            ).start()
        return carry

    lax.fori_loop(0, 18, spread, 0)

    @pl.when(me < 18)
    def _():
        parts[me] = pieces[me]
        others = parts.at[0 : BAND - 1]
        wait(others, power_recv)
        column = 128 * lax.rem(me, 3) + lax.broadcasted_iota(jnp.int32, (8, 128), 1)
        value = jnp.sum(parts[...], axis=0) / (2 * column + 1).astype(F32)
        result[...] = value
        final[me] = value

        def share(o, carry):
            pltpu.make_async_remote_copy(
                src_ref=result, dst_ref=final.at[me], send_sem=final_send, recv_sem=final_recv,
                device_id={"band": lax.rem(me + o, BAND)}, device_id_type=MESH,
            ).start()
            return carry

        lax.fori_loop(1, BAND, share, 0)
        wait(final.at[0:17], final_recv)
        wait(others, final_send)
        wait(pieces.at[0:17], power_send)

    @pl.when(me >= 18)
    def _():
        wait(final, final_recv)
        wait(pieces, power_send)

    for j in range(18):
        g, t = j // 3, j % 3
        width = 128 if t < 2 else 64
        energy_ref[8 * g : 8 * g + 8, 128 * t : 128 * t + width] = final[j][:, :width]

    for g in range(groups):
        wait(send_a.at[g, 0 : BAND - 1], sent_a.at[g])
        wait(send_b.at[g, 0 : BAND - 1], sent_b.at[g])
    if short:
        for c, over in ((0, over_a), (1, over_b)):
            wait(over.at[0:7, 0], hop1_sent.at[c])
            wait(over.at[:, 0:3], hop2_sent.at[c])
    for g in range(4):
        pltpu.make_async_copy(spec.at[5 * g : 5 * g + 5], spec_ref.at[5 * g : 5 * g + 5], spec_sem.at[g]).wait()


def fused(short, starts, row_latitude, row_points, rows, legendre, pick):
    groups = 2 if short else 4
    smem = pl.BlockSpec(memory_space=pltpu.SMEM)
    vmem = pl.BlockSpec(memory_space=pltpu.VMEM)
    hbm = pl.BlockSpec(memory_space=pl.ANY)
    dma = pltpu.SemaphoreType.DMA
    return pl.pallas_call(
        functools.partial(fused_kernel, short),
        in_specs=[smem, smem, smem, hbm, hbm, vmem],
        out_specs=[hbm, vmem],
        out_shape=[
            jax.ShapeDtypeStruct((CAP, 2 * F, NN), F32),
            jax.ShapeDtypeStruct((F, NN), F32),
        ],
        scratch_shapes=[
            pltpu.VMEM((ROWS, F, 1280), F32),
            pltpu.VMEM((10, F, 128), F32),
            pltpu.VMEM((CAP, NN, NLATH), BF16),
            pltpu.VMEM((768, 256), BF16),
            pltpu.VMEM((384, 768), BF16),
            pltpu.VMEM((384, 768), BF16),
            pltpu.VMEM((LT, 8, 128), F32),
            pltpu.VMEM((LT, 16, 128), F32),
            pltpu.VMEM((groups, BAND, 32, 128), BF16),
            pltpu.VMEM((groups, BAND, 48, 128), BF16),
            pltpu.VMEM((groups, BAND, 32, 128), BF16),
            pltpu.VMEM((groups, BAND, 48, 128), BF16),
            pltpu.VMEM((8, 4, 2, 32, 128), BF16),
            pltpu.VMEM((8, 4, 2, 48, 128), BF16),
            pltpu.VMEM((CAP, 640, NN), BF16),
            pltpu.VMEM((512, 640), BF16),
            pltpu.VMEM((CAP, 2 * F, NN), F32),
            pltpu.VMEM((F, 384), F32),
            pltpu.VMEM((18, 8, 128), F32),
            pltpu.VMEM((BAND, 8, 128), F32),
            pltpu.VMEM((8, 128), F32),
            pltpu.VMEM((18, 8, 128), F32),
            dma((ROWS,)), dma, dma((4,)),
            dma((groups,)), dma((groups,)), dma((groups,)), dma((groups,)),
            dma((2,)), dma((2,)), dma((2,)), dma((2,)),
            dma, dma, dma, dma,
        ],
        compiler_params=pltpu.CompilerParams(
            collective_id=0 if short else 1, has_side_effects=True, vmem_limit_bytes=VMEM
        ),
        name="short" if short else "full",
    )(starts, row_latitude, row_points, rows, legendre, pick)


def on_device(grid, row_points, row_latitude, order_owner, legendre):
    bands = jnp.arange(BAND + 1, dtype=jnp.int32)
    starts = jnp.sum((order_owner[None, :] < bands[:, None]).astype(jnp.int32), axis=1)
    crowded = starts[1:] - starts[:-1] > SHORT
    over = jnp.max(jnp.where(crowded, starts[:-1] + SHORT, 0))
    few = jnp.sum(crowded.astype(jnp.int32)) <= 1
    starts = jnp.concatenate([starts, over[None]])
    by_device = row_latitude.reshape(BAND, ROWS)
    stacked = jnp.concatenate([by_device[:, a:b].reshape(-1) for a, b in ((0, 8), (8, 16), (16, 20))])
    column = jnp.where(stacked < NLATH, stacked, 2 * NLATH - 1 - stacked)
    pick = (column[:, None] == jnp.arange(NLATH, dtype=jnp.int32)[None, :]).astype(BF16)
    rows = jnp.transpose(grid, (1, 0, 2))
    spectral, energy = lax.cond(
        few, functools.partial(fused, True), functools.partial(fused, False),
        starts, row_latitude, row_points, rows, legendre, pick,
    )
    return spectral.reshape(CAP, 2, F, NN), energy


def solution(mesh):
    in_specs = (P("member", "band", None), P(), P(), P(), P("band", None, None))
    out_specs = (P("band", None, "member", None), P("member", None))
    return jax.shard_map(
        on_device, mesh=mesh, in_specs=in_specs, out_specs=out_specs, check_vma=False
    )
```

time: 119 us -> 80.3 us (0.67)
  Pallas kernels: 110 us -> 72.8 us
  local copies, waits for them, and re-layouts: 5.36 us -> 3.47 us
    pallas_call x2 -> x1, Pallas kernels: 110 us -> 72.8 us  [fused(): pl.pallas_call(functools.partial(fused_kernel, short), in_specs=[smem, sm...]
    unnamed x5 -> x4, local copies, waits for them, and re-layouts: 4.31 us -> 2.24 us
where the time goes in v2:
time: 80.3 us; the launch traced here: 80.1 us
  Pallas kernels  72.8 us (91%)
  local copies, waits for them, and re-layouts  3.47 us (4%)
  other arithmetic  2.39 us (3%)
  between operations  1.34 us (2%)
    pallas_call x1, Pallas kernels, fused(): pl.pallas_call(functools.partial(fused_kernel, short), in_specs=[smem, sm...  72.8 us
    unnamed x4, local copies, waits for them, and re-layouts  2.24 us

profile of v2, /device:TPU:2, one launch (start us, length us, event | category | flops | bytes accessed | tf_op | source)
XLA Modules:
  0.0 80.1 jit_solution(7585515447252191848)
XLA Ops:
  0.6 0.8 convert_reduce_fusion
  1.4 0.7 fusion.2
  2.8 0.7 pad_add_fusion
  3.5 0.8 reshape.81
  4.3 0.1 slice.23
  4.4 0.1 concatenate.25
  4.5 0.1 fusion.3
  4.6 0.1 concatenate.24
  4.7 0.1 concatenate.23
  4.8 0.2 fusion
  5.0 72.9 %conditional.1 = (f32[48,320]{1,0:T(8,128)S(1)}, f32[20,2,48,320]{3,2,1,0:T(8,128)S(1)}) conditional(s32[]{:T(128)} %convert_element_type.14, (s32[34]{0:T(128)S(1)}, s32[640]{0:T(1024)}, s32[640]{0:T(1024)}, f32[20,48,1280]{2,1,0:T(8,128)}, bf16[20,320,320]{2,1,0:T(8,128)(2,1)}, /*index=5*/bf16[640,320]{1,0:T(8,128)(2,1)S(1)}) %tuple.26, ...), branch_computations={%region_3.4_spmd, %region_4.5_spmd} | conditional | bytes 16 | solution.py:444
  5.0 72.8 %short.1 = (f32[20,96,320]{2,1,0:T(8,128)S(1)}, f32[48,320]{1,0:T(8,128)S(1)}) custom-call(s32[34]{0:T(128)S(1)} %get-tuple-element.37.start_ref, s32[640]{0:T(1024)} %get-tuple-element.38.lat_ref, s32[640]{0:T(1024)} %get-tuple-element.39.points_ref, f32[20,48,1280]{2,1,0:T(8,128)} %get-tuple-element.40.grid_ref, ...), custom_call_target="tpu_custom_call" | custom-call | tf_op jit(solution)/shard_map/cond/branch_1_fun/short/pallas_call | solution.py:389
  77.8 1.6 %copy.16 = f32[20,2,48,320]{3,2,1,0:T(8,128)} copy(f32[20,2,48,320]{3,2,1,0:T(8,128)S(1)} %get-tuple-element.61) | data formatting | bytes 4915200
  79.4 0.6 copy.17
  (5 shorter events, 0.0 us)

commit v3 on v2

--- a/solution.py
+++ b/solution.py
@@ -128,35 +128,36 @@
         f_ref[pl.ds(t, 80, stride=3), slot, :] = kept
 
 
-def take_orders(f_ref, order, height):
+def take_orders(f_ref, order):
     order = jnp.minimum(order, NN)
     rest = (96 * order) & 127
-    tiles = f_ref[pl.ds((3 * order) >> 2, 5)].reshape(5 * height, 128)
+    tiles = f_ref[pl.ds((3 * order) >> 2, 5)].reshape(40, 128)
     rolled = pltpu.roll(tiles, (128 - rest) & 127, axis=1)
-    here = lax.broadcasted_iota(jnp.int32, (height, 128), 1) < 128 - rest
-    cut = [rolled[height * j : height * (j + 1)] for j in range(5)]
+    here = lax.broadcasted_iota(jnp.int32, (8, 128), 1) < 128 - rest
+    cut = [rolled[8 * j : 8 * j + 8] for j in range(5)]
     return [jnp.where(here, cut[j], cut[j + 1]) for j in range(4)]
 
 
-def pack_a(f_ref, order):
-    return jnp.concatenate(take_orders(f_ref, order, 8), axis=0).astype(BF16)
-
-
-def pack_b(f_ref, order):
-    v = take_orders(f_ref, order, 16)
+def pack_eight(f_ref, order):
+    return jnp.concatenate(take_orders(f_ref, order), axis=0).astype(BF16)
+
+
+def pack_four(f_ref, order):
+    v = take_orders(f_ref, order)
     low = lax.broadcasted_iota(jnp.int32, (8, 128), 0) < 4
-    tails = [jnp.where(low, v[j][8:], pltpu.roll(v[j + 1][8:], 4, axis=0)) for j in (0, 2)]
-    return jnp.concatenate([v[j][:8] for j in range(4)] + tails, axis=0).astype(BF16)
+    return jnp.concatenate(
+        [jnp.where(low, v[j], pltpu.roll(v[j + 1], 4, axis=0)) for j in (0, 2)], axis=0
+    ).astype(BF16)
 
 
 def octets(block):
-    wide = block.astype(F32).reshape(BAND, 4, 8, 128)
-    return [wide[:, a].reshape(256, 128).T.astype(BF16) for a in range(4)]
+    wide = block.astype(F32).reshape(16, 4, 8, 128)
+    return [wide[:, a].reshape(128, 128).T.astype(BF16) for a in range(4)]
 
 
 def quads(block):
-    wide = block.astype(F32).reshape(16, 2, 2, 8, 128)
-    low = lax.broadcasted_iota(jnp.int32, (16, 8, 128), 1) < 4
+    wide = block.astype(F32).reshape(8, 2, 2, 8, 128)
+    low = lax.broadcasted_iota(jnp.int32, (8, 8, 128), 1) < 4
     out = []
     for a in range(4):
         even, odd = wide[:, 0, a // 2], wide[:, 1, a // 2]
@@ -164,7 +165,7 @@
             tail = jnp.where(low, even, pltpu.roll(odd, 4, axis=1))
         else:
             tail = jnp.where(low, pltpu.roll(even, 4, axis=1), odd)
-        out.append(tail.reshape(128, 128).T.astype(BF16))
+        out.append(tail.reshape(64, 128).T.astype(BF16))
     return out
 
 
@@ -172,24 +173,43 @@
     pltpu.make_async_copy(ref, ref, sem).wait()
 
 
+def far_first(i):
+    a, b = i // 4, lax.rem(i, 4)
+    dz = jnp.where(lax.rem(a, 2) == 1, 4 - (a + 1) // 2, 4 + a // 2)
+    dy = jnp.where(lax.rem(b, 2) == 1, 2 - (b + 1) // 2, 2 + b // 2)
+    return dz, dy
+
+
+CHUNKS = ((0, 4, 256), (4, 8, 0), (12, 8, 128))
+
+
 def fused_kernel(short, start_ref, lat_ref, points_ref, grid_ref, leg_hbm, pick_ref, spec_ref, energy_ref,
-                 x_ref, tile_ref, leg_ref, w_ref, bhi_ref, blo_ref, fa_ref, fb_ref,
-                 send_a, send_b, recv_a, recv_b, over_a, over_b,
-                 lp, xt, spec, power, pieces, parts, result, final,
-                 x_sem, leg_sem, spec_sem, sent_a, sent_b, got_a, got_b,
+                 x_ref, tile_ref, leg_ref, w_ref, bhi_ref, blo_ref, f_ref,
+                 send_0, send_1, send_2, recv_0, recv_1, recv_2, over_0, over_1, over_2,
+                 lp, xt_n, xt_s, spec, power, pieces, parts, result, final,
+                 x_sem, leg_sem, spec_sem, sent, got,
                  hop1_sent, hop1_got, hop2_sent, hop2_got,
                  power_send, power_recv, final_send, final_recv):
     groups = 2 if short else 4
+    send, recv, over = (send_0, send_1, send_2), (recv_0, recv_1, recv_2), (over_0, over_1, over_2)
     me = lax.axis_index("band")
     z, y = me // 4, lax.rem(me, 4)
+    place = jnp.where(me < 16, me, 47 - me)
     barrier = pltpu.get_barrier_semaphore()
 
     def greet(o, carry):
         pl.semaphore_signal(barrier, inc=1, device_id={"band": lax.rem(me + o, BAND)}, device_id_type=MESH)
         return carry
 
+    def peer_of(i):
+        dz, dy = far_first(i)
+        return lax.rem(z + dz, 8) * 4 + lax.rem(y + dy, 4)
+
+    def stored(r):
+        return jnp.where(me < 16, r, ROWS - 1 - r)
+
     def load(r):
-        return pltpu.make_async_copy(grid_ref.at[r], x_ref.at[r], x_sem.at[r])
+        return pltpu.make_async_copy(grid_ref.at[stored(r)], x_ref.at[r], x_sem.at[r])
 
     def load_row(r, carry):
         load(r).start()
@@ -200,72 +220,85 @@
     leg_copy = pltpu.make_async_copy(leg_hbm, leg_ref, leg_sem)
     leg_copy.start()
 
-    fa_ref[240:] = jnp.zeros((8, 8, 128), F32)
-    fb_ref[240:] = jnp.zeros((8, 16, 128), F32)
+    f_ref[240:] = jnp.zeros((8, 8, 128), F32)
     zero = jnp.zeros((F, 384), BF16)
     for ref in (bhi_ref, blo_ref):
         ref[0:48, 384:768] = zero
         ref[48:96, 0:384] = zero
 
-    def dft(first, f_ref):
+    def crowd(d, carry):
+        first = start_ref[d]
+        return carry + jnp.where(start_ref[d + 1] - first > SHORT, first + SHORT, 0)
+
+    extra = lax.fori_loop(0, BAND, crowd, 0) if short else None
+
+    def dft_chunk(c):
+        first, rows, _ = CHUNKS[c]
+
         def body(r, carry):
             load(r).wait()
-            length = points_ref[lat_ref[me * ROWS + r]]
+            length = points_ref[lat_ref[me * ROWS + stored(r)]]
             dft_row(x_ref, tile_ref, r, length, w_ref, bhi_ref, blo_ref, f_ref, r - first)
             return carry
-        return body
-
-    def pack_all(packer, f_ref, send, recv, over):
-        def body(d, carry):
-            for g in range(groups):
-                send[g, d] = packer(f_ref, start_ref[d] + 5 * g)
-            return carry
-        lax.fori_loop(0, BAND, body, 0)
-        for g in range(groups):
-            recv[g, me] = send[g, me]
+
+        lax.fori_loop(first, first + rows, body, 0)
+        packer = pack_four if rows == 4 else pack_eight
         if short:
             for j in range(2):
-                over[z, y, j] = packer(f_ref, start_ref[BAND + 1] + 5 * j)
-
-    def send_all(c, send, recv, over, sent, got):
+                over[c][z, y, j] = packer(f_ref, extra + 5 * j)
+
+        def pack(d, carry):
+            for g in range(groups):
+                send[c][d, g] = packer(f_ref, start_ref[d] + 5 * g)
+            return carry
+
+        lax.fori_loop(0, BAND, pack, 0, unroll=4)
+        recv[c][place] = send[c][me]
+
+    def send_chunk(c):
         if short:
             def hop1(o, carry):
                 pltpu.make_async_remote_copy(
-                    src_ref=over.at[z, y], dst_ref=over.at[z, y],
+                    src_ref=over[c].at[z, y], dst_ref=over[c].at[z, y],
                     send_sem=hop1_sent.at[c], recv_sem=hop1_got.at[c],
                     device_id={"band": lax.rem(z + o, 8) * 4 + y}, device_id_type=MESH,
                 ).start()
                 return carry
             lax.fori_loop(1, 8, hop1, 0)
-        for g in range(groups):
-            def body(o, carry, g=g):
-                peer = lax.rem(me + o, BAND)
-                pltpu.make_async_remote_copy(
-                    src_ref=send.at[g, peer], dst_ref=recv.at[g, me],
-                    send_sem=sent.at[g], recv_sem=got.at[g],
-                    device_id={"band": peer}, device_id_type=MESH,
-                ).start()
-                return carry
-            lax.fori_loop(1, BAND, body, 0)
-
-    def forward(c, over):
-        wait(over.at[0:7, 0], hop1_got.at[c])
+
+        def body(i, carry):
+            peer = peer_of(i)
+            pltpu.make_async_remote_copy(
+                src_ref=send[c].at[peer], dst_ref=recv[c].at[place],
+                send_sem=sent.at[c], recv_sem=got.at[c],
+                device_id={"band": peer}, device_id_type=MESH,
+            ).start()
+            return carry
+
+        lax.fori_loop(0, BAND - 1, body, 0)
+
+    def forward(c):
+        if not short:
+            return
+        wait(over[c].at[0:7, 0], hop1_got.at[c])
+
         def hop2(o, carry):
             pltpu.make_async_remote_copy(
-                src_ref=over.at[:, y], dst_ref=over.at[:, y],
+                src_ref=over[c].at[:, y], dst_ref=over[c].at[:, y],
                 send_sem=hop2_sent.at[c], recv_sem=hop2_got.at[c],
                 device_id={"band": z * 4 + lax.rem(y + o, 4)}, device_id_type=MESH,
             ).start()
             return carry
         lax.fori_loop(1, 4, hop2, 0)
 
-    lax.fori_loop(0, 8, dft(0, fa_ref), 0)
-    pack_all(pack_a, fa_ref, send_a, recv_a, over_a)
+    dft_chunk(0)
     pl.semaphore_wait(barrier, BAND - 1)
-    send_all(0, send_a, recv_a, over_a, sent_a, got_a)
-    lax.fori_loop(8, ROWS, dft(8, fb_ref), 0)
-    pack_all(pack_b, fb_ref, send_b, recv_b, over_b)
-    send_all(1, send_b, recv_b, over_b, sent_b, got_b)
+    send_chunk(0)
+    dft_chunk(1)
+    send_chunk(1)
+    forward(0)
+    dft_chunk(2)
+    send_chunk(2)
     leg_copy.wait()
 
     start = start_ref[me]
@@ -273,48 +306,39 @@
     degree = lax.broadcasted_iota(jnp.int32, (1, NN), 1)
 
     def permute(s, carry):
-        sign = (1 - 2 * ((degree + start + s) & 1)).astype(F32)
-        value = lax.dot_general(
+        lp[s] = lax.dot_general(
             pick_ref[...], leg_ref[s], (((1,), (1,)), ((), ())), preferred_element_type=F32
-        )
-        for at, size, south in ((0, 128, 0), (128, 128, 1), (256, 128, 0), (384, 128, 1), (512, 64, 0), (576, 64, 1)):
-            piece = value[at : at + size]
-            lp[s, at : at + size, :] = (piece * sign if south else piece).astype(BF16)
+        ).astype(BF16)
         return carry
 
-    lax.fori_loop(0, SHORT, permute, 0)
-    if short:
-        forward(0, over_a)
-    lax.fori_loop(SHORT, CAP, permute, 0)
-    if short:
-        forward(1, over_b)
+    lax.fori_loop(0, 2, permute, 0, unroll=2)
+    forward(1)
+    lax.fori_loop(2, SHORT, permute, 0, unroll=2)
+    forward(2)
+    lax.fori_loop(SHORT, CAP, permute, 0, unroll=2)
     power[...] = jnp.zeros_like(power)
 
     for g in range(4):
-        if g < groups:
-            wait(recv_a.at[g, 0 : BAND - 1], got_a.at[g])
-            block_a = recv_a[g]
-        else:
-            if g == groups:
-                wait(over_a.at[:, 0:3], hop2_got.at[0])
-            block_a = over_a[:, :, g - groups].reshape(BAND, 32, 128)
-        for a, value in enumerate(octets(block_a)):
-            xt[128 * a : 128 * a + 128, 0:256] = value
-        if g < groups:
-            wait(recv_b.at[g, 0 : BAND - 1], got_b.at[g])
-            block_b = recv_b[g]
-        else:
-            if g == groups:
-                wait(over_b.at[:, 0:3], hop2_got.at[1])
-            block_b = over_b[:, :, g - groups].reshape(BAND, 48, 128)
-        for a, value in enumerate(octets(block_b[:, 0:32])):
-            xt[128 * a : 128 * a + 128, 256:512] = value
-        for a, value in enumerate(quads(block_b[:, 32:48])):
-            xt[128 * a : 128 * a + 128, 512:640] = value
+        for c, (_, rows, at) in enumerate(CHUNKS):
+            if g < groups:
+                if g == 0:
+                    wait(recv[c].at[0 : BAND - 1], got.at[c])
+                north, south = recv[c][0:16, g], recv[c][16:32, g]
+            else:
+                if g == groups:
+                    wait(over[c].at[:, 0:3], hop2_got.at[c])
+                block = over[c][:, :, g - groups].reshape(BAND, 4 * rows, 128)
+                north, south = block[0:16], jnp.stack([block[BAND - 1 - d] for d in range(16)])
+            for ref, block in ((xt_n, north), (xt_s, south)):
+                for a, value in enumerate(quads(block) if rows == 4 else octets(block)):
+                    ref[128 * a : 128 * a + 128, at : at + 16 * rows] = value
         for i in range(5):
             s = 5 * g + i
             order = start + s
-            value = jnp.dot(xt[96 * i : 96 * i + 96, :], lp[s], preferred_element_type=F32)
+            both = jnp.concatenate([xt_n[96 * i : 96 * i + 96, :], xt_s[96 * i : 96 * i + 96, :]], axis=0)
+            value = jnp.dot(both, lp[s], preferred_element_type=F32)
+            sign = (1 - 2 * ((degree + order) & 1)).astype(F32)
+            value = value[0:96] + sign * value[96:192]
             first = jnp.where(s < count, order, NN)
             value = jnp.where(degree >= first, value, 0.0)
             spec[s] = value
@@ -326,16 +350,18 @@
     for j in range(18):
         pieces[j] = power[8 * (j // 3) : 8 * (j // 3) + 8, 128 * (j % 3) : 128 * (j % 3) + 128]
 
-    def spread(j, carry):
-        @pl.when(j != me)
+    def spread(i, carry):
+        peer = peer_of(i)
+
+        @pl.when(peer < 18)
         def _():
             pltpu.make_async_remote_copy(
-                src_ref=pieces.at[j], dst_ref=parts.at[me], send_sem=power_send, recv_sem=power_recv,
-                device_id={"band": j}, device_id_type=MESH,
+                src_ref=pieces.at[peer], dst_ref=parts.at[me], send_sem=power_send, recv_sem=power_recv,
+                device_id={"band": peer}, device_id_type=MESH,
             ).start()
         return carry
 
-    lax.fori_loop(0, 18, spread, 0)
+    lax.fori_loop(0, BAND - 1, spread, 0)
 
     @pl.when(me < 18)
     def _():
@@ -347,14 +373,14 @@
         result[...] = value
         final[me] = value
 
-        def share(o, carry):
+        def share(i, carry):
             pltpu.make_async_remote_copy(
                 src_ref=result, dst_ref=final.at[me], send_sem=final_send, recv_sem=final_recv,
-                device_id={"band": lax.rem(me + o, BAND)}, device_id_type=MESH,
+                device_id={"band": peer_of(i)}, device_id_type=MESH,
             ).start()
             return carry
 
-        lax.fori_loop(1, BAND, share, 0)
+        lax.fori_loop(0, BAND - 1, share, 0)
         wait(final.at[0:17], final_recv)
         wait(others, final_send)
         wait(pieces.at[0:17], power_send)
@@ -369,13 +395,11 @@
         width = 128 if t < 2 else 64
         energy_ref[8 * g : 8 * g + 8, 128 * t : 128 * t + width] = final[j][:, :width]
 
-    for g in range(groups):
-        wait(send_a.at[g, 0 : BAND - 1], sent_a.at[g])
-        wait(send_b.at[g, 0 : BAND - 1], sent_b.at[g])
-    if short:
-        for c, over in ((0, over_a), (1, over_b)):
-            wait(over.at[0:7, 0], hop1_sent.at[c])
-            wait(over.at[:, 0:3], hop2_sent.at[c])
+    for c in range(3):
+        wait(send[c].at[0 : BAND - 1], sent.at[c])
+        if short:
+            wait(over[c].at[0:7, 0], hop1_sent.at[c])
+            wait(over[c].at[:, 0:3], hop2_sent.at[c])
     for g in range(4):
         pltpu.make_async_copy(spec.at[5 * g : 5 * g + 5], spec_ref.at[5 * g : 5 * g + 5], spec_sem.at[g]).wait()
 
@@ -402,15 +426,11 @@
             pltpu.VMEM((384, 768), BF16),
             pltpu.VMEM((384, 768), BF16),
             pltpu.VMEM((LT, 8, 128), F32),
-            pltpu.VMEM((LT, 16, 128), F32),
-            pltpu.VMEM((groups, BAND, 32, 128), BF16),
-            pltpu.VMEM((groups, BAND, 48, 128), BF16),
-            pltpu.VMEM((groups, BAND, 32, 128), BF16),
-            pltpu.VMEM((groups, BAND, 48, 128), BF16),
-            pltpu.VMEM((8, 4, 2, 32, 128), BF16),
-            pltpu.VMEM((8, 4, 2, 48, 128), BF16),
-            pltpu.VMEM((CAP, 640, NN), BF16),
-            pltpu.VMEM((512, 640), BF16),
+            *[pltpu.VMEM((BAND, groups, 4 * rows, 128), BF16) for _, rows, _ in CHUNKS * 2],
+            *[pltpu.VMEM((8, 4, 2, 4 * rows, 128), BF16) for _, rows, _ in CHUNKS],
+            pltpu.VMEM((CAP, NLATH, NN), BF16),
+            pltpu.VMEM((512, NLATH), BF16),
+            pltpu.VMEM((512, NLATH), BF16),
             pltpu.VMEM((CAP, 2 * F, NN), F32),
             pltpu.VMEM((F, 384), F32),
             pltpu.VMEM((18, 8, 128), F32),
@@ -418,8 +438,7 @@
             pltpu.VMEM((8, 128), F32),
             pltpu.VMEM((18, 8, 128), F32),
             dma((ROWS,)), dma, dma((4,)),
-            dma((groups,)), dma((groups,)), dma((groups,)), dma((groups,)),
-            dma((2,)), dma((2,)), dma((2,)), dma((2,)),
+            dma((3,)), dma((3,)), dma((3,)), dma((3,)), dma((3,)), dma((3,)),
             dma, dma, dma, dma,
         ],
         compiler_params=pltpu.CompilerParams(
@@ -433,12 +452,10 @@
     bands = jnp.arange(BAND + 1, dtype=jnp.int32)
     starts = jnp.sum((order_owner[None, :] < bands[:, None]).astype(jnp.int32), axis=1)
     crowded = starts[1:] - starts[:-1] > SHORT
-    over = jnp.max(jnp.where(crowded, starts[:-1] + SHORT, 0))
     few = jnp.sum(crowded.astype(jnp.int32)) <= 1
-    starts = jnp.concatenate([starts, over[None]])
-    by_device = row_latitude.reshape(BAND, ROWS)
-    stacked = jnp.concatenate([by_device[:, a:b].reshape(-1) for a, b in ((0, 8), (8, 16), (16, 20))])
-    column = jnp.where(stacked < NLATH, stacked, 2 * NLATH - 1 - stacked)
+    northern = row_latitude[:NLATH].reshape(BAND // 2, ROWS)
+    ordered = sorted(CHUNKS, key=lambda chunk: chunk[2])
+    column = jnp.concatenate([northern[:, first : first + rows].reshape(-1) for first, rows, _ in ordered])
     pick = (column[:, None] == jnp.arange(NLATH, dtype=jnp.int32)[None, :]).astype(BF16)
     rows = jnp.transpose(grid, (1, 0, 2))
     spectral, energy = lax.cond(

time: 80.3 us -> 74.3 us (0.925)
  Pallas kernels: 72.8 us -> 67.2 us
    pallas_call x1, Pallas kernels: 72.8 us -> 67.2 us  [fused(): pl.pallas_call(functools.partial(fused_kernel, short), in_specs=[smem, sm...]
    unnamed x4 -> x2, local copies, waits for them, and re-layouts: 2.24 us -> 2.23 us
where the time goes in v3:
time: 74.3 us; the launch traced here: 73.9 us
  Pallas kernels  67.2 us (90%)
  local copies, waits for them, and re-layouts  3.34 us (4%)
  other arithmetic  1.63 us (2%)
  between operations  1.32 us (2%)
    pallas_call x1, Pallas kernels, fused(): pl.pallas_call(functools.partial(fused_kernel, short), in_specs=[smem, sm...  67.2 us
    unnamed x2, local copies, waits for them, and re-layouts  2.23 us

profile of v3, /device:TPU:2, one launch (start us, length us, event | category | flops | bytes accessed | tf_op | source)
XLA Modules:
  0.0 73.9 jit_solution(8324569005695411363)
XLA Ops:
  0.6 0.8 %convert_reduce_fusion = s32[33]{0:T(128)S(1)} fusion(s32[320]{0:T(512)} %param.10), kind=kLoop, calls=%fused_computation.2 | loop fusion | flops 31647 | bytes 1412 | tf_op jit(solution)/shard_map/reduce_sum | solution.py:453
  1.4 0.7 fusion.1
  2.8 0.7 slice.28
  3.5 0.1 reshape.33
  3.6 0.1 reshape.36
  3.7 0.1 fusion.2
  3.7 0.1 reshape.34
  3.8 0.1 reshape.35
  3.9 0.1 fusion
  4.1 67.6 %conditional.1 = (f32[48,320]{1,0:T(8,128)S(1)}, f32[20,2,48,320]{3,2,1,0:T(8,128)S(1)}) conditional(s32[]{:T(128)} %convert_element_type.14, (s32[33]{0:T(128)S(1)}, s32[640]{0:T(1024)}, s32[640]{0:T(1024)}, f32[20,48,1280]{2,1,0:T(8,128)}, bf16[20,320,320]{2,1,0:T(8,128)(2,1)}, /*index=5*/bf16[320,320]{1,0:T(8,128)(2,1)S(1)}) %tuple.25, ...), branch_computations={%region_2.0_spmd, %region_3.0_spmd} | conditional | bytes 16 | solution.py:461
  4.3 67.2 %short.1 = (f32[20,96,320]{2,1,0:T(8,128)S(1)}, f32[48,320]{1,0:T(8,128)S(1)}) custom-call(s32[33]{0:T(128)S(1)} %get-tuple-element.37.start_ref, s32[640]{0:T(1024)} %get-tuple-element.38.lat_ref, s32[640]{0:T(1024)} %get-tuple-element.39.points_ref, f32[20,48,1280]{2,1,0:T(8,128)} %get-tuple-element.40.grid_ref, ...), custom_call_target="tpu_custom_call" | custom-call | tf_op jit(solution)/shard_map/cond/branch_1_fun/short/pallas_call | solution.py:413
  71.7 1.6 %copy.13 = f32[20,2,48,320]{3,2,1,0:T(8,128)} copy(f32[20,2,48,320]{3,2,1,0:T(8,128)S(1)} %get-tuple-element.59) | data formatting | bytes 4915200
  73.3 0.6 copy.14
  (1 shorter events, 0.0 us)

commit v4 on v3

--- a/solution.py
+++ b/solution.py
@@ -43,7 +43,7 @@
     return hi, (x - hi.astype(F32)).astype(BF16)
 
 
-def dft_row(x_ref, tile_ref, r, length, w_ref, bhi_ref, blo_ref, f_ref, slot):
+def dft_row(x_ref, tile_ref, r, length, w_ref, b_ref, f_ref, slot):
     quarter = length // 4
     for t in range(10):
         tile_ref[t] = x_ref[r, :, 128 * t : 128 * t + 128]
@@ -70,9 +70,8 @@
         for part in range(2):
             value = jnp.concatenate([tiles[a][part], tiles[a + 1][part]], axis=0) * scale
             hi, lo = split(value)
-            at = part * 384 + 8 * a
-            w_ref[at : at + 16, 0:128] = hi
-            w_ref[at : at + 16, 128:256] = lo
+            for at, piece in ((8 * a, hi), (384 + 8 * a, lo), (768 + 8 * a, hi)):
+                w_ref[at : at + 16, 128 * part : 128 * part + 128] = piece
 
     psub = lax.broadcasted_iota(jnp.int32, (8, 384), 0)
     plane = lax.broadcasted_iota(jnp.int32, (8, 384), 1)
@@ -106,19 +105,20 @@
             (y2 * c2, -(y2 * s2)),
             (o0 * c3 + o1 * s3, o1 * c3 - o0 * s3),
         ]
-        for p, (zr, zi) in enumerate(pairs):
-            top, mid = 96 * p, 96 * p + 48
-            for ref, value in zip((bhi_ref, blo_ref), split(zr)):
-                ref[top : top + 48, lo_at:hi_at] = value
-                ref[mid : mid + 48, 384 + lo_at : 384 + hi_at] = -value
-            if zi is not None:
-                for ref, value in zip((bhi_ref, blo_ref), split(zi)):
-                    ref[top : top + 48, 384 + lo_at : 384 + hi_at] = value
-                    ref[mid : mid + 48, lo_at:hi_at] = value
-
-    first = jnp.dot(bhi_ref[...], w_ref[...], preferred_element_type=F32)
-    second = jnp.dot(blo_ref[...], w_ref[:, 0:128], preferred_element_type=F32)
-    total = first[:, 0:128] + first[:, 128:256] + second
+        row = 0
+        for value in (v for pair in pairs for v in pair if v is not None):
+            hi, lo = split(value)
+            for at, piece in ((0, hi), (384, hi), (768, lo)):
+                b_ref[row : row + 48, at + lo_at : at + hi_at] = piece
+            row += 48
+
+    sums = jnp.dot(b_ref[...], w_ref[...], preferred_element_type=F32)
+    cosine = [sums[48 * i : 48 * i + 48, 0:128] for i in range(7)]
+    sine = [sums[48 * i : 48 * i + 48, 128:256] for i in range(7)]
+    blocks = [cosine[0], -sine[0]]
+    for i in (1, 3, 5):
+        blocks += [cosine[i] + sine[i + 1], cosine[i + 1] - sine[i]]
+    total = jnp.concatenate(blocks, axis=0)
     for t in range(3):
         turned = total[128 * t : 128 * t + 128].T[:80]
         k = lax.broadcasted_iota(jnp.int32, (80, 128), 0)
@@ -184,7 +184,7 @@
 
 
 def fused_kernel(short, start_ref, lat_ref, points_ref, grid_ref, leg_hbm, pick_ref, spec_ref, energy_ref,
-                 x_ref, tile_ref, leg_ref, w_ref, bhi_ref, blo_ref, f_ref,
+                 x_ref, tile_ref, leg_ref, w_ref, b_ref, f_ref,
                  send_0, send_1, send_2, recv_0, recv_1, recv_2, over_0, over_1, over_2,
                  lp, xt_n, xt_s, spec, power, pieces, parts, result, final,
                  x_sem, leg_sem, spec_sem, sent, got,
@@ -221,10 +221,6 @@
     leg_copy.start()
 
     f_ref[240:] = jnp.zeros((8, 8, 128), F32)
-    zero = jnp.zeros((F, 384), BF16)
-    for ref in (bhi_ref, blo_ref):
-        ref[0:48, 384:768] = zero
-        ref[48:96, 0:384] = zero
 
     def crowd(d, carry):
         first = start_ref[d]
@@ -238,7 +234,7 @@
         def body(r, carry):
             load(r).wait()
             length = points_ref[lat_ref[me * ROWS + stored(r)]]
-            dft_row(x_ref, tile_ref, r, length, w_ref, bhi_ref, blo_ref, f_ref, r - first)
+            dft_row(x_ref, tile_ref, r, length, w_ref, b_ref, f_ref, r - first)
             return carry
 
         lax.fori_loop(first, first + rows, body, 0)
@@ -275,7 +271,7 @@
             ).start()
             return carry
 
-        lax.fori_loop(0, BAND - 1, body, 0)
+        lax.fori_loop(0, BAND - 1, body, 0, unroll=31)
 
     def forward(c):
         if not short:
@@ -361,7 +357,7 @@
             ).start()
         return carry
 
-    lax.fori_loop(0, BAND - 1, spread, 0)
+    lax.fori_loop(0, BAND - 1, spread, 0, unroll=31)
 
     @pl.when(me < 18)
     def _():
@@ -380,7 +376,7 @@
             ).start()
             return carry
 
-        lax.fori_loop(0, BAND - 1, share, 0)
+        lax.fori_loop(0, BAND - 1, share, 0, unroll=31)
         wait(final.at[0:17], final_recv)
         wait(others, final_send)
         wait(pieces.at[0:17], power_send)
@@ -422,9 +418,8 @@
             pltpu.VMEM((ROWS, F, 1280), F32),
             pltpu.VMEM((10, F, 128), F32),
             pltpu.VMEM((CAP, NN, NLATH), BF16),
-            pltpu.VMEM((768, 256), BF16),
-            pltpu.VMEM((384, 768), BF16),
-            pltpu.VMEM((384, 768), BF16),
+            pltpu.VMEM((1152, 256), BF16),
+            pltpu.VMEM((336, 1152), BF16),
             pltpu.VMEM((LT, 8, 128), F32),
             *[pltpu.VMEM((BAND, groups, 4 * rows, 128), BF16) for _, rows, _ in CHUNKS * 2],
             *[pltpu.VMEM((8, 4, 2, 4 * rows, 128), BF16) for _, rows, _ in CHUNKS],

time: 74.3 us -> 72.6 us (0.977)
  Pallas kernels: 67.2 us -> 65.7 us
    pallas_call x1, Pallas kernels: 67.2 us -> 65.7 us  [fused(): pl.pallas_call(functools.partial(fused_kernel, short), in_specs=[smem, sm...]
where the time goes in v4:
time: 72.6 us; the launch traced here: 72.4 us
  Pallas kernels  65.7 us (90%)
  local copies, waits for them, and re-layouts  3.34 us (5%)
  other arithmetic  1.63 us (2%)
  between operations  1.32 us (2%)
    pallas_call x1, Pallas kernels, fused(): pl.pallas_call(functools.partial(fused_kernel, short), in_specs=[smem, sm...  65.7 us
    unnamed x2, local copies, waits for them, and re-layouts  2.23 us

profile of v4, /device:TPU:2, one launch (start us, length us, event | category | flops | bytes accessed | tf_op | source)
XLA Modules:
  0.0 72.4 jit_solution(16735586513578953043)
XLA Ops:
  0.6 0.8 %convert_reduce_fusion = s32[33]{0:T(128)S(1)} fusion(s32[320]{0:T(512)} %param.10), kind=kLoop, calls=%fused_computation.2 | loop fusion | flops 31647 | bytes 1412 | tf_op jit(solution)/shard_map/reduce_sum | solution.py:448
  1.4 0.7 fusion.1
  2.8 0.7 slice.28
  3.5 0.1 reshape.33
  3.6 0.1 reshape.36
  3.7 0.1 fusion.2
  3.7 0.1 reshape.34
  3.8 0.1 reshape.35
  3.9 0.1 fusion
  4.1 66.1 %conditional.1 = (f32[48,320]{1,0:T(8,128)S(1)}, f32[20,2,48,320]{3,2,1,0:T(8,128)S(1)}) conditional(s32[]{:T(128)} %convert_element_type.14, (s32[33]{0:T(128)S(1)}, s32[640]{0:T(1024)}, s32[640]{0:T(1024)}, f32[20,48,1280]{2,1,0:T(8,128)}, bf16[20,320,320]{2,1,0:T(8,128)(2,1)}, /*index=5*/bf16[320,320]{1,0:T(8,128)(2,1)S(1)}) %tuple.25, ...), branch_computations={%region_2.0_spmd, %region_3.0_spmd} | conditional | bytes 16 | solution.py:456
  4.3 65.7 %short.1 = (f32[20,96,320]{2,1,0:T(8,128)S(1)}, f32[48,320]{1,0:T(8,128)S(1)}) custom-call(s32[33]{0:T(128)S(1)} %get-tuple-element.37.start_ref, s32[640]{0:T(1024)} %get-tuple-element.38.lat_ref, s32[640]{0:T(1024)} %get-tuple-element.39.points_ref, f32[20,48,1280]{2,1,0:T(8,128)} %get-tuple-element.40.grid_ref, ...), custom_call_target="tpu_custom_call" | custom-call | tf_op jit(solution)/shard_map/cond/branch_1_fun/short/pallas_call | solution.py:409
  70.2 1.6 %copy.13 = f32[20,2,48,320]{3,2,1,0:T(8,128)} copy(f32[20,2,48,320]{3,2,1,0:T(8,128)S(1)} %get-tuple-element.59) | data formatting | bytes 4915200
  71.8 0.6 copy.14
  (1 shorter events, 0.0 us)
